TPU v7x, 32 devices: a whole 2x2x4 slice. The times are simulated.
32 devices in a mesh: expert: 4 (over y, x), shard: 8 (over z, core).
Axes of the slice: x: 2, y: 2, z: 4, core: 2. Of those that a mesh axis runs over, the one named last changes fastest.
Arguments:
- tokens: bfloat16 [512, 4096], P('expert', 'shard'), may hold values from -6 to 6
- routes: int32 [512, 2], P('expert'), may hold values from 0 to 3, all different within a row; in each aligned block of 128 rows (0 to 127, 128 to 255, ...) at most 128 rows name the same one
- mix_weights: float32 [512, 2], P('expert'), may hold values from 0.1 to 1
- cotangent: bfloat16 [512, 4096], P('expert', 'shard'), may hold values from -6 to 6
- w_gate: bfloat16 [4, 4096, 6144], P('expert', 'shard'), may hold values from -0.09375 to 0.09375
- w_up: bfloat16 [4, 4096, 6144], P('expert', 'shard'), may hold values from -0.09375 to 0.09375
- w_down: bfloat16 [4, 4096, 6144], P('expert', 'shard'), may hold values from -0.078125 to 0.078125
Outputs:
- layer_out: bfloat16 [512, 4096], P('expert', 'shard')
- grad_tokens: bfloat16 [512, 4096], P('expert', 'shard')
- grad_gate: bfloat16 [4, 4096, 6144], P('expert', None, 'shard')
- grad_up: bfloat16 [4, 4096, 6144], P('expert', None, 'shard')
- grad_down: bfloat16 [4, 4096, 6144], P('expert', None, 'shard')
Inputs may be any that keep to these rules, and one draw needn't show every extreme that they name: `routes`: each token names two different experts. Among the 128 tokens of one block, no expert is named by more than 128 tokens, and in every draw some expert is named by exactly 128 tokens of some block. Every expert is named by some token.
All inputs are finite; a program needn't handle non-finite values.
Results may differ from a plain program's by a relative error of at most 0.015.
Values may be sent and summed in bfloat16 or wider, within the bound.
A program may use at most 128 MiB of HBM per device.

v0:
```python
import jax
import jax.numpy as jnp
from jax import lax
from jax.sharding import PartitionSpec as P


def slot_targets(routes, capacity, experts):
    flat_routes = routes.reshape(-1)
    expert_iota = jnp.arange(experts, dtype=jnp.int32)
    one_hot = (flat_routes[:, None] == expert_iota[None, :]).astype(jnp.int32)
    earlier = jnp.cumsum(one_hot, axis=0) - one_hot
    slot_number = jnp.sum(earlier * one_hot, axis=1)
    return (flat_routes * capacity + slot_number).reshape(routes.shape)


def feature_total(partial_value):
    return lax.psum_scatter(
        partial_value.astype(jnp.bfloat16), "shard", scatter_dimension=1, tiled=True
    )


def send_home(row_block, experts, capacity):
    shaped = row_block.reshape(experts, capacity, row_block.shape[1])
    returned = lax.all_to_all(shaped, "expert", split_axis=0, concat_axis=0, tiled=True)
    return returned.reshape(experts * capacity, row_block.shape[1])


def local(tokens, routes, mix_weights, cotangent, w_gate, w_up, w_down):
    experts = lax.axis_size("expert")
    tok_dev = tokens.shape[0]
    capacity = min(tok_dev, 6 * tok_dev // experts)
    target = slot_targets(routes, capacity, experts)
    slot_iota = jnp.arange(experts * capacity, dtype=jnp.int32)
    slot_hits = slot_iota[:, None, None] == target[None, :, :]
    picker = jnp.sum(slot_hits.astype(jnp.float32), axis=2).astype(jnp.bfloat16)
    slot_weight = jnp.sum(jnp.where(slot_hits, mix_weights[None, :, :], 0.0), axis=(1, 2))
    gate_own, up_own, down_own = (
        lax.all_to_all(w_gate, "shard", split_axis=2, concat_axis=1, tiled=True),
        lax.all_to_all(w_up, "shard", split_axis=2, concat_axis=1, tiled=True),
        lax.all_to_all(w_down, "shard", split_axis=2, concat_axis=1, tiled=True),
    )
    gate_own = gate_own[0]
    up_own = up_own[0]
    down_own = down_own[0]
    piece_width = tokens.shape[1]
    row_send = jnp.dot(picker, tokens, preferred_element_type=jnp.float32).astype(jnp.bfloat16)
    grad_send = (
        jnp.dot(picker, cotangent, preferred_element_type=jnp.float32) * slot_weight[:, None]
    ).astype(jnp.bfloat16)
    row_send = row_send.reshape(experts, capacity, piece_width)
    grad_send = grad_send.reshape(experts, capacity, piece_width)
    row_part, grad_part = (
        lax.all_to_all(row_send, "expert", split_axis=0, concat_axis=0, tiled=True),
        lax.all_to_all(grad_send, "expert", split_axis=0, concat_axis=0, tiled=True),
    )
    row_recv, grad_recv = (
        lax.all_gather(row_part, "shard", axis=2, tiled=True),
        lax.all_gather(grad_part, "shard", axis=2, tiled=True),
    )
    model_width = row_recv.shape[2]
    x_rows = row_recv.reshape(-1, model_width)
    dy_rows = grad_recv.reshape(-1, model_width)
    gate_pre = jnp.dot(x_rows, gate_own, preferred_element_type=jnp.float32)
    up_pre = jnp.dot(x_rows, up_own, preferred_element_type=jnp.float32)
    sigmoid_gate = jax.nn.sigmoid(gate_pre)
    active = gate_pre * sigmoid_gate
    hidden = (active * up_pre).astype(jnp.bfloat16)
    down_part = lax.dot_general(
        hidden, down_own, (((1,), (1,)), ((), ())), preferred_element_type=jnp.float32
    )
    out_home = send_home(feature_total(down_part), experts, capacity)
    picked = out_home[target]
    layer_out = jnp.sum(mix_weights[:, :, None] * picked.astype(jnp.float32), axis=1).astype(
        jnp.bfloat16
    )
    d_hidden = jnp.dot(dy_rows, down_own, preferred_element_type=jnp.float32)
    d_gate = (d_hidden * up_pre * sigmoid_gate * (1.0 + gate_pre * (1.0 - sigmoid_gate))).astype(
        jnp.bfloat16
    )
    d_up = (d_hidden * active).astype(jnp.bfloat16)
    row_contract = (((0,), (0,)), ((), ()))
    grad_down = lax.dot_general(
        dy_rows, hidden, row_contract, preferred_element_type=jnp.float32
    ).astype(jnp.bfloat16)
    grad_gate = lax.dot_general(
        x_rows, d_gate, row_contract, preferred_element_type=jnp.float32
    ).astype(jnp.bfloat16)
    grad_up = lax.dot_general(
        x_rows, d_up, row_contract, preferred_element_type=jnp.float32
    ).astype(jnp.bfloat16)
    col_contract = (((1,), (1,)), ((), ()))
    dx_part = lax.dot_general(d_gate, gate_own, col_contract, preferred_element_type=jnp.float32)
    dx_part = dx_part + lax.dot_general(
        d_up, up_own, col_contract, preferred_element_type=jnp.float32
    )
    dx_home = send_home(feature_total(dx_part), experts, capacity)
    grad_tokens = jnp.sum(dx_home[target].astype(jnp.float32), axis=1).astype(jnp.bfloat16)
    return (layer_out, grad_tokens, grad_gate[None], grad_up[None], grad_down[None])


def solution(mesh):
    return jax.shard_map(
        local,
        mesh=mesh,
        in_specs=(
            P("expert", "shard"),
            P("expert", None),
            P("expert", None),
            P("expert", "shard"),
            P("expert", "shard", None),
            P("expert", "shard", None),
            P("expert", "shard", None),
        ),
        out_specs=(
            P("expert", "shard"),
            P("expert", "shard"),
            P("expert", None, "shard"),
            P("expert", None, "shard"),
            P("expert", None, "shard"),
        ),
        check_vma=False,
    )
```

profile of v0, /device:TPU:0, one launch (start us, length us, event | category | flops | bytes accessed | tf_op | source)
XLA Modules:
  0.0 797.6 jit_solution(13853023410183731343)
XLA Ops:
  7.2 0.8 copy.68
  8.0 0.1 eq.43
  8.1 0.1 eq.39
  8.3 1.2 reduce-window.6
  9.6 0.1 copy.70
  9.9 0.1 reduce_sum.51
  10.1 0.7 compare_select_fusion
  10.9 0.8 select_reduce_fusion
  11.7 1.1 fusion.4
  12.8 5.2 all-to-all-start.5
  18.0 2.0 convolution_convert_fusion.4
  19.9 6.0 all-to-all-done.5
  26.0 3.5 all-to-all-start
  29.5 26.8 %copy.73 = bf16[1,512,6144]{1,0,2:T(2,128)(2,1)} copy(bf16[1,512,6144]{2,1,0:T(8,128)(2,1)} %param.11) | data formatting | bytes 12582912 | tf_op args[4]
  56.2 0.5 broadcast.51
  56.8 41.7 %reduce.2 = bf16[6144,512]{1,0:T(8,128)(2,1)} reduce(bf16[6144,1,512]{2,1,0:T(2,128)(2,1)} %bitcast.76, bf16[]{:T(256)} %broadcast.51), dimensions={1}, to_apply=%bitcast.47.reduce_sub_computation | reduce | bytes 12582914
  98.4 9.3 %reshape.98 = bf16[8,2,196608]{2,1,0:T(2,128)(2,1)} reshape(bf16[6144,512]{1,0:T(8,128)(2,1)} %reduce.2) | data formatting | bytes 12582912
  107.8 0.8 copy-done.3
  108.6 4.9 all-to-all-start.1
  113.4 26.8 %copy.75 = bf16[1,512,6144]{1,0,2:T(2,128)(2,1)} copy(bf16[1,512,6144]{2,1,0:T(8,128)(2,1)} %param.12) | data formatting | bytes 12582912 | tf_op args[5]
  140.2 41.7 %reduce.3 = bf16[6144,512]{1,0:T(8,128)(2,1)} reduce(bf16[6144,1,512]{2,1,0:T(2,128)(2,1)} %bitcast.78, bf16[]{:T(256)} %broadcast.51), dimensions={1}, to_apply=%bitcast.45.reduce_sub_computation | reduce | bytes 12582914
  181.9 9.3 %reshape.96 = bf16[8,2,196608]{2,1,0:T(2,128)(2,1)} reshape(bf16[6144,512]{1,0:T(8,128)(2,1)} %reduce.3) | data formatting | bytes 12582912
  191.2 61.3 %all-to-all-done.1 = bf16[8,2,196608]{2,1,0:T(2,128)(2,1)} async-done(((bf16[8,2,196608]{2,1,0:T(2,128)(2,1)}), bf16[8,2,196608]{2,1,0:T(2,128)(2,1)}, u32[]{:S(2)}, u32[]{:S(2)}) %all-to-all-start.1) | async-done | bytes 6291488 | tf_op jit(solution)/shard_map/all_to_all | solution.py:38
  252.5 4.8 all-to-all-start.2
  257.3 0.5 all-gather.3.cloned.1.call-start
  257.8 0.2 all-gather.3.cloned.1.call-update
  258.0 26.9 %copy.77 = bf16[1,512,6144]{1,0,2:T(2,128)(2,1)} copy(bf16[1,512,6144]{2,1,0:T(8,128)(2,1)} %param.13) | data formatting | bytes 12582912 | tf_op args[6]
  284.9 41.7 %reduce.4 = bf16[6144,512]{1,0:T(8,128)(2,1)} reduce(bf16[6144,1,512]{2,1,0:T(2,128)(2,1)} %bitcast.77, bf16[]{:T(256)} %broadcast.51), dimensions={1}, to_apply=%bitcast.49.reduce_sub_computation | reduce | bytes 12582914
  326.6 9.4 %reshape.100 = bf16[8,2,196608]{2,1,0:T(2,128)(2,1)} reshape(bf16[6144,512]{1,0:T(8,128)(2,1)} %reduce.4) | data formatting | bytes 12582912
  336.0 94.0 %all-to-all-done.2 = bf16[8,2,196608]{2,1,0:T(2,128)(2,1)} async-done(((bf16[8,2,196608]{2,1,0:T(2,128)(2,1)}), bf16[8,2,196608]{2,1,0:T(2,128)(2,1)}, u32[]{:S(2)}, u32[]{:S(2)}) %all-to-all-start.2) | async-done | bytes 6291488 | tf_op jit(solution)/shard_map/all_to_all | solution.py:39
  429.9 4.8 all-to-all-start.3
  434.8 0.7 all-gather.5.cloned.1.call-update
  435.5 11.0 %reshape.99 = bf16[6144,1,512]{2,1,0:T(2,128)(2,1)} reshape(bf16[8,2,196608]{2,1,0:T(2,128)(2,1)} %all-to-all-done.1) | data formatting | bytes 12582912
  446.5 9.5 %copy.80 = bf16[1,512,6144]{1,2,0:T(8,128)(2,1)} copy(bf16[1,512,6144]{1,0,2:T(2,128)(2,1)} %bitcast.73) | data formatting | bytes 12582912
  456.0 8.6 %copy.74 = bf16[1,8,512,768]{3,2,1,0:T(8,128)(2,1)} copy(bf16[1,8,512,768]{2,3,1,0:T(8,128)(2,1)} %bitcast.79) | data formatting | bytes 12582912 | tf_op jit(solution)/shard_map/all_to_all | solution.py:38
  464.6 11.0 %reshape.97 = bf16[6144,1,512]{2,1,0:T(2,128)(2,1)} reshape(bf16[8,2,196608]{2,1,0:T(2,128)(2,1)} %all-to-all-done.2) | data formatting | bytes 12582912
  475.6 9.2 %copy.81 = bf16[1,512,6144]{1,2,0:T(8,128)(2,1)} copy(bf16[1,512,6144]{1,0,2:T(2,128)(2,1)} %bitcast.74) | data formatting | bytes 12582912
  484.8 8.6 %copy.76 = bf16[1,8,512,768]{3,2,1,0:T(8,128)(2,1)} copy(bf16[1,8,512,768]{2,3,1,0:T(8,128)(2,1)} %bitcast.80) | data formatting | bytes 12582912 | tf_op jit(solution)/shard_map/all_to_all | solution.py:39
  493.5 113.9 %all-to-all-done.3 = bf16[8,2,196608]{2,1,0:T(2,128)(2,1)} async-done(((bf16[8,2,196608]{2,1,0:T(2,128)(2,1)}), bf16[8,2,196608]{2,1,0:T(2,128)(2,1)}, u32[]{:S(2)}, u32[]{:S(2)}) %all-to-all-start.3) | async-done | bytes 6291488 | tf_op jit(solution)/shard_map/all_to_all | solution.py:40
  607.4 11.0 %reshape.101 = bf16[6144,1,512]{2,1,0:T(2,128)(2,1)} reshape(bf16[8,2,196608]{2,1,0:T(2,128)(2,1)} %all-to-all-done.3) | data formatting | bytes 12582912
  618.3 9.1 %copy.82 = bf16[1,512,6144]{1,2,0:T(8,128)(2,1)} copy(bf16[1,512,6144]{1,0,2:T(2,128)(2,1)} %bitcast.75) | data formatting | bytes 12582912
  627.5 8.9 %copy.78 = bf16[1,8,512,768]{3,2,1,0:T(8,128)(2,1)} copy(bf16[1,8,512,768]{2,3,1,0:T(8,128)(2,1)} %bitcast.81) | data formatting | bytes 12582912 | tf_op jit(solution)/shard_map/all_to_all | solution.py:40
  636.5 8.7 %fusion.10 = f32[512,768]{1,0:T(8,128)} fusion(bf16[512,4096]{1,0:T(8,128)(2,1)} %bitcast.95, bf16[4096,768]{1,0:T(8,128)(2,1)} %bitcast.84), kind=kOutput, calls=%fused_computation.34 | convolution fusion | flops 3221225472 | bytes 12058624 | tf_op jit(solution)/shard_map/dot_general | solution.py:63
  645.2 4.6 fusion.11
  649.8 8.7 %multiply_convert_fusion = (bf16[512,768]{1,0:T(8,128)(2,1)S(1)}, bf16[512,768]{1,0:T(8,128)(2,1)S(1)}, bf16[512,768]{1,0:T(8,128)(2,1)S(1)}) fusion(f32[512,768]{1,0:T(8,128)} %fusion.10, f32[512,768]{1,0:T(8,128)} %fusion.11, bf16[512,4096]{1,0:T(8,128)(2,1)} %bitcast.99, bf16[4096,768]{1,0:T(8,128)(2,1)} %bitcast.86), kind=kOutput, calls=%fused_computation.10 | convolution fusion | flops 3227123712 | bytes 15990784 | tf_op jit(solution)/shard_map/dot_general | solution.py:76
  658.5 5.9 fusion.12
  664.4 8.0 %add_convert_fusion = bf16[512,4096]{1,0:T(8,128)(2,1)} fusion(f32[512,4096]{1,0:T(8,128)S(1)} %fusion.12, bf16[512,768]{1,0:T(8,128)(2,1)S(1)} %get-tuple-element.9, bf16[4096,768]{1,0:T(8,128)(2,1)} %bitcast.88), kind=kOutput, calls=%fused_computation.2 | convolution fusion | flops 3225419776 | bytes 19660800 | tf_op jit(solution)/shard_map/dot_general | solution.py:93
  672.5 8.0 %convolution_convert_fusion.3 = bf16[512,4096]{1,0:T(8,128)(2,1)} fusion(bf16[512,768]{1,0:T(8,128)(2,1)S(1)} %get-tuple-element.11, bf16[4096,768]{1,0:T(8,128)(2,1)} %bitcast.87), kind=kOutput, calls=%fused_computation.9 | convolution fusion | flops 3223322624 | bytes 11272192 | tf_op jit(solution)/shard_map/dot_general | solution.py:68
  680.5 0.1 copy.67
  680.6 0.1 copy.79
  680.7 0.1 reshape.77
  680.9 8.5 %fusion.2 = bf16[1,4096,768]{2,1,0:T(8,128)(2,1)} fusion(bf16[512,4096]{1,0:T(8,128)(2,1)} %bitcast.100, bf16[512,768]{1,0:T(8,128)(2,1)S(1)} %get-tuple-element.11), kind=kOutput, calls=%fused_computation.8 | convolution fusion | flops 3224371200 | bytes 11272192 | tf_op jit(solution)/shard_map/dot_general | solution.py:82
  689.4 32.6 %reduce-scatter.5.cloned.1.call-done = bf16[512,512]{1,0:T(8,128)(2,1)} async-done(((bf16[512,4096]{1,0:T(8,128)(2,1)}), bf16[512,512]{1,0:T(8,128)(2,1)}) %reduce-scatter.5.cloned.1.call-update) | async-done | bytes 524304 | tf_op jit(solution)/shard_map/reduce_scatter | solution.py:17
  721.9 3.7 all-to-all-start.6
  725.6 8.4 %fusion = bf16[1,4096,768]{2,1,0:T(8,128)(2,1)} fusion(bf16[512,4096]{1,0:T(8,128)(2,1)} %bitcast.96, bf16[512,768]{1,0:T(8,128)(2,1)S(1)} %copy-done.7), kind=kOutput, calls=%fused_computation.6 | convolution fusion | flops 3224371200 | bytes 11272192 | tf_op jit(solution)/shard_map/dot_general | solution.py:85
  734.0 38.9 %reduce-scatter.3.cloned.1.call-done = bf16[512,512]{1,0:T(8,128)(2,1)} async-done(((bf16[512,4096]{1,0:T(8,128)(2,1)}), bf16[512,512]{1,0:T(8,128)(2,1)}) %reduce-scatter.3.cloned.1.call-update) | async-done | bytes 524304 | tf_op jit(solution)/shard_map/reduce_scatter | solution.py:17
  772.8 3.9 all-to-all-start.4
  776.8 8.4 %fusion.1 = bf16[1,4096,768]{2,1,0:T(8,128)(2,1)} fusion(bf16[512,4096]{1,0:T(8,128)(2,1)} %bitcast.97, bf16[512,768]{1,0:T(8,128)(2,1)S(1)} %get-tuple-element.9), kind=kOutput, calls=%fused_computation.7 | convolution fusion | flops 3224371200 | bytes 11272192 | tf_op jit(solution)/shard_map/dot_general | solution.py:88
  785.2 1.2 gather_fusion.1
  786.3 0.1 reshape.88
  786.5 1.2 gather_fusion
  787.6 0.3 reshape.95
  787.9 1.4 reduce_sum.55
  789.3 1.4 multiply_reduce_fusion
  (39 shorter events, 0.6 us)
Async XLA Ops:
  7.2 4.5 copy-start
  12.8 13.2 %all-to-all-start.5 = ((bf16[4,128,512]{2,1,0:T(8,128)(2,1)}), bf16[4,128,512]{2,1,0:T(8,128)(2,1)S(1)}, u32[]{:S(2)}, u32[]{:S(2)}) async-start(bf16[4,128,512]{2,1,0:T(8,128)(2,1)} %bitcast.12), calls=%async_computation.6 | async-start | bytes 1048576 | tf_op jit(solution)/shard_map/all_to_all | solution.py:54
  26.0 30.3 %copy-start.2 = (bf16[4,128,512]{2,1,0:T(8,128)(2,1)}, bf16[4,128,512]{2,1,0:T(8,128)(2,1)S(1)}, u32[]{:S(2)}) copy-start(bf16[4,128,512]{2,1,0:T(8,128)(2,1)S(1)} %all-to-all-done.5) | copy-start | bytes 1572868
  26.0 81.8 %all-to-all-start = ((bf16[4,128,512]{2,1,0:T(8,128)(2,1)}), bf16[4,128,512]{2,1,0:T(8,128)(2,1)S(1)}, u32[]{:S(2)}, u32[]{:S(2)}) async-start(bf16[4,128,512]{2,1,0:T(8,128)(2,1)} %bitcast.2), calls=%async_computation | async-start | bytes 1048576 | tf_op jit(solution)/shard_map/all_to_all | solution.py:53
  107.8 0.8 copy-start.3
  108.6 143.9 %all-to-all-start.1 = ((bf16[8,2,196608]{2,1,0:T(2,128)(2,1)}), bf16[8,2,196608]{2,1,0:T(2,128)(2,1)}, u32[]{:S(2)}, u32[]{:S(2)}) async-start(bf16[8,2,196608]{2,1,0:T(2,128)(2,1)} %reshape.98), calls=%async_computation.1 | async-start | bytes 12582912 | tf_op jit(solution)/shard_map/all_to_all | solution.py:38
  252.5 177.4 %all-to-all-start.2 = ((bf16[8,2,196608]{2,1,0:T(2,128)(2,1)}), bf16[8,2,196608]{2,1,0:T(2,128)(2,1)}, u32[]{:S(2)}, u32[]{:S(2)}) async-start(bf16[8,2,196608]{2,1,0:T(2,128)(2,1)} %reshape.96), calls=%async_computation.2 | async-start | bytes 12582912 | tf_op jit(solution)/shard_map/all_to_all | solution.py:39
  257.3 379.2 %all-gather.3.cloned.1.call-start = ((), (), s32[]{:S(2)}) async-start(), calls=%async_computation.9 | async-start | bytes 4718592 | tf_op jit(solution)/shard_map/all_gather | solution.py:57
  429.9 177.5 %all-to-all-start.3 = ((bf16[8,2,196608]{2,1,0:T(2,128)(2,1)}), bf16[8,2,196608]{2,1,0:T(2,128)(2,1)}, u32[]{:S(2)}, u32[]{:S(2)}) async-start(bf16[8,2,196608]{2,1,0:T(2,128)(2,1)} %reshape.100), calls=%async_computation.3 | async-start | bytes 12582912 | tf_op jit(solution)/shard_map/all_to_all | solution.py:40
  434.7 215.1 %all-gather.5.cloned.1.call-start = ((), (), s32[]{:S(2)}) async-start(), calls=%async_computation.11 | async-start | bytes 4718592 | tf_op jit(solution)/shard_map/all_gather | solution.py:58
  435.5 286.4 %reduce-scatter.5.cloned.1.call-start = ((), (), s32[]{:S(2)}) async-start(), calls=%async_computation.12 | async-start | bytes 4718592 | tf_op jit(solution)/shard_map/reduce_scatter | solution.py:17
  627.5 17.7 %slice-start = ((s8[6291456]{0:T(1024)(128)(4,1)}), s8[2097152]{0:T(1024)(128)(4,1)S(1)}, s32[]{:S(2)}) async-start(s8[6291456]{0:T(1024)(128)(4,1)} %bitcast.89), calls=%async_computation.13 | async-start | bytes 4194304
  636.4 8.8 %slice-start.1 = ((s8[6291456]{0:T(1024)(128)(4,1)}), s8[4194304]{0:T(1024)(128)(4,1)S(1)}, s32[]{:S(2)}) async-start(s8[6291456]{0:T(1024)(128)(4,1)} %bitcast.89), calls=%async_computation.14 | async-start | bytes 8388608
  636.5 8.8 %copy-start.5 = (bf16[4,128,4096]{2,1,0:T(8,128)(2,1)S(1)}, bf16[4,128,4096]{2,1,0:T(8,128)(2,1)}, u32[]{:S(2)}) copy-start(bf16[4,128,4096]{2,1,0:T(8,128)(2,1)} %all-gather.3.cloned.1.call-done) | copy-start | bytes 12582916
  658.5 5.9 copy-start.6
  672.4 100.4 %reduce-scatter.3.cloned.1.call-start = ((), (), s32[]{:S(2)}) async-start(), calls=%async_computation.10 | async-start | bytes 4718592 | tf_op jit(solution)/shard_map/reduce_scatter | solution.py:17
  672.5 8.0 %copy-start.4 = (f32[128,2]{0,1:T(2,128)S(1)}, f32[128,2]{0,1:T(2,128)}, u32[]{:S(2)}) copy-start(f32[128,2]{0,1:T(2,128)} %param.9) | copy-start | bytes 3076
  680.9 44.7 %copy-start.7 = (bf16[512,768]{1,0:T(8,128)(2,1)S(1)}, bf16[512,768]{1,0:T(8,128)(2,1)}, u32[]{:S(2)}) copy-start(bf16[512,768]{1,0:T(8,128)(2,1)} %copy-done.6) | copy-start | bytes 2359300
  721.9 50.9 %all-to-all-start.6 = ((bf16[4,128,512]{2,1,0:T(8,128)(2,1)}), bf16[4,128,512]{2,1,0:T(8,128)(2,1)S(1)}, u32[]{:S(2)}, u32[]{:S(2)}) async-start(bf16[4,128,512]{2,1,0:T(8,128)(2,1)} %bitcast.93), calls=%async_computation.8 | async-start | bytes 1048576 | tf_op jit(solution)/shard_map/all_to_all | solution.py:24
  772.8 13.6 %all-to-all-start.4 = ((bf16[4,128,512]{2,1,0:T(8,128)(2,1)}), bf16[4,128,512]{2,1,0:T(8,128)(2,1)S(1)}, u32[]{:S(2)}, u32[]{:S(2)}) async-start(bf16[4,128,512]{2,1,0:T(8,128)(2,1)} %bitcast.92), calls=%async_computation.5 | async-start | bytes 1048576 | tf_op jit(solution)/shard_map/all_to_all | solution.py:24
  776.7 13.9 %copy-start.1 = (bf16[128,512]{1,0:T(8,128)(2,1)S(1)}, bf16[128,512]{1,0:T(8,128)(2,1)}, u32[]{:S(2)}) copy-start(bf16[128,512]{1,0:T(8,128)(2,1)} %param.10) | copy-start | bytes 393220
Sparse Core Ops, SparseCore 0:
  259.7 85.6 all-gather.2
  437.2 85.6 all-gather.4
  672.5 49.3 reduce-scatter.4
  724.6 48.1 reduce-scatter.2
where the time goes:
time: 809 us; the launch traced here: 798 us
  waiting for transfers between devices  348 us (43%)
  local copies, waits for them, and re-layouts  202 us (25%)
  other arithmetic  131 us (16%)
  matrix products  72.2 us (9%)
  starting transfers between devices  31.3 us (4%)
  between operations  14.4 us (2%)
    unnamed x35, local copies, waits for them, and re-layouts  172 us
    unnamed x5, other arithmetic  125 us
    all_to_all x1, waiting for transfers between devices, local(): lax.all_to_all(w_down, 'shard', split_axis=2, concat_axis=1, tiled=True)  114 us
    all_to_all x1, waiting for transfers between devices, local(): lax.all_to_all(w_up, 'shard', split_axis=2, concat_axis=1, tiled=True)  94 us
    reduce_scatter x2, waiting for transfers between devices, feature_total(): lax.psum_scatter(partial_value.astype(jnp.bfloat16), 'shard', scatter_dim...  71.4 us
    all_to_all x1, waiting for transfers between devices, local(): lax.all_to_all(w_gate, 'shard', split_axis=2, concat_axis=1, tiled=True)  61.3 us
  transfers between devices with their start and end apart: 11, of which 6 were waited for; matrix products, arithmetic and copies ran while one was open for 47% of the time, Pallas kernels for 0%

commit v1 on v0

v1 whole, which is shorter than its diff:
```python
import functools

import jax
import jax.numpy as jnp
from jax import lax
from jax.experimental import pallas as pl
from jax.experimental.pallas import tpu as pltpu
from jax.sharding import PartitionSpec as P

MESH = pl.DeviceIdType.MESH
VMEM_BUDGET = 56 * 1024 * 1024
ROW_CUTS = 2


def place(shards):
    me = lax.axis_index("shard")
    chip = me // 2
    core = me % 2
    return me, chip, core, me + 1 - 2 * core


def greet(me, chip, sibling, line):
    barrier = pltpu.get_barrier_semaphore()
    pl.semaphore_signal(barrier, inc=1, device_id={"shard": sibling}, device_id_type=MESH)

    @pl.when(chip > 0)
    def _():
        pl.semaphore_signal(barrier, inc=1, device_id={"shard": me - 2}, device_id_type=MESH)

    @pl.when(chip < line - 1)
    def _():
        pl.semaphore_signal(barrier, inc=1, device_id={"shard": me + 2}, device_id_type=MESH)

    peers = jnp.where(chip > 0, 2, 1) + jnp.where(chip < line - 1, 1, 0)
    pl.semaphore_wait(barrier, peers)


def scatter_sum_kernel(
    shards, cuts, p0, p1, p2, out, stage, core_in, line_in,
    load_sem, core_send, core_recv, line_send, line_recv,
):
    line = shards // 2
    units, _, rows, width = stage.shape
    me, chip, core, sibling = place(shards)
    order = sorted(range(line), key=lambda d: -abs(2 * d - line + 1))
    greet(me, chip, sibling, line)

    def load(part, u, r, d):
        cols = pl.ds(pl.multiple_of((2 * d + core) * width, 128), width)
        return pltpu.make_async_copy(
            part.at[pl.ds(r * rows, rows), cols], stage.at[u, d], load_sem.at[u, d]
        )

    def swap(part, u, r, d):
        cols = pl.ds(pl.multiple_of((2 * d + 1 - core) * width, 128), width)
        return pltpu.make_async_remote_copy(
            src_ref=part.at[pl.ds(r * rows, rows), cols],
            dst_ref=core_in.at[u, d],
            send_sem=core_send.at[u, d],
            recv_sem=core_recv.at[u, d],
            device_id={"shard": sibling},
            device_id_type=MESH,
        )

    def pass_on(u, d, slot, to):
        return pltpu.make_async_remote_copy(
            src_ref=stage.at[u, d],
            dst_ref=line_in.at[u, slot],
            send_sem=line_send.at[u, d],
            recv_sem=line_recv.at[u, slot],
            device_id={"shard": to},
            device_id_type=MESH,
        )

    for m, part in enumerate((p0, p1, p2)):
        def begin(r, carry, m=m, part=part):
            u = m * cuts + r
            for d in order:
                swap(part, u, r, d).start()
                load(part, u, r, d).start()
            return carry

        lax.fori_loop(0, cuts, begin, 0)

    def wide(ref):
        return ref[...].astype(jnp.float32)

    def relay(u, carry):
        for d in order:
            @pl.when(chip != d)
            def _(d=d):
                rightward = chip < d
                slot = jnp.where(rightward, d + 1, d)
                to = jnp.where(rightward, me + 2, me - 2)
                load(p0, u, 0, d).wait()
                swap(p0, u, 0, d).wait_recv()
                at_end = jnp.where(rightward, chip == 0, chip == line - 1)

                @pl.when(at_end)
                def _():
                    stage[u, d] = (wide(stage.at[u, d]) + wide(core_in.at[u, d])).astype(
                        stage.dtype
                    )

                @pl.when(jnp.logical_not(at_end))
                def _():
                    pass_on(u, d, slot, to).wait_recv()
                    stage[u, d] = (
                        wide(stage.at[u, d]) + wide(core_in.at[u, d]) + wide(line_in.at[u, slot])
                    ).astype(stage.dtype)

                pass_on(u, d, slot, to).start()
        return carry

    lax.fori_loop(0, units, relay, 0)

    def finish(u, carry):
        load(p0, u, 0, chip).wait()
        swap(p0, u, 0, chip).wait_recv()
        out[u] = wide(stage.at[u, chip]) + wide(core_in.at[u, chip])

        @pl.when(chip > 0)
        def _():
            pass_on(u, chip, chip + 1, sibling).wait_recv()
            out[u] += wide(line_in.at[u, chip + 1])

        @pl.when(chip < line - 1)
        def _():
            pass_on(u, chip, chip, sibling).wait_recv()
            out[u] += wide(line_in.at[u, chip])

        for d in range(line):
            swap(p0, u, 0, d).wait_send()

            @pl.when(chip != d)
            def _(d=d):
                pass_on(u, d, d, sibling).wait_send()
        return carry

    lax.fori_loop(0, units, finish, 0)


def scatter_sum(shards, parts):
    rows_all, cols = parts[0].shape
    rows, width, line = rows_all // ROW_CUTS, cols // shards, shards // 2
    units = 3 * ROW_CUTS
    dma = pltpu.SemaphoreType.DMA
    out = pl.pallas_call(
        functools.partial(scatter_sum_kernel, shards, ROW_CUTS),
        out_shape=jax.ShapeDtypeStruct((units, rows, width), jnp.float32),
        in_specs=[pl.BlockSpec(memory_space=pl.ANY)] * 3,
        out_specs=pl.BlockSpec(memory_space=pltpu.VMEM),
        scratch_shapes=[
            pltpu.VMEM((units, line, rows, width), jnp.bfloat16),
            pltpu.VMEM((units, line, rows, width), jnp.bfloat16),
            pltpu.VMEM((units, line + 1, rows, width), jnp.bfloat16),
            dma((units, line)),
            dma((units, line)),
            dma((units, line)),
            dma((units, line)),
            dma((units, line + 1)),
        ],
        compiler_params=pltpu.CompilerParams(
            collective_id=0, has_side_effects=True, vmem_limit_bytes=VMEM_BUDGET
        ),
        cost_estimate=pl.CostEstimate(
            flops=100_000_000_000, bytes_accessed=500_000_000, transcendentals=0
        ),
    )(*parts)
    return out.reshape(3, rows_all, width)


def gather_kernel(shards, cuts, a, b, c, full, own_sem, line_right, line_left, line_recv, core_send, core_recv):
    line = shards // 2
    rows_all, width = a.shape
    rows = rows_all // cuts
    units = 3 * cuts
    me, chip, core, sibling = place(shards)
    greet(me, chip, sibling, line)

    def block(u, shard):
        return full.at[
            pl.ds(u * rows, rows), pl.ds(pl.multiple_of(shard * width, 128), width)
        ]

    def send(src, u, origin, way):
        shard = 2 * origin + core
        return pltpu.make_async_remote_copy(
            src_ref=src,
            dst_ref=block(u, shard),
            send_sem=(line_right if way > 0 else line_left).at[u, origin],
            recv_sem=line_recv.at[u, origin],
            device_id={"shard": me + 2 * way},
            device_id_type=MESH,
        )

    def share(src, u, origin):
        return pltpu.make_async_remote_copy(
            src_ref=src,
            dst_ref=block(u, 2 * origin + core),
            send_sem=core_send.at[u, origin],
            recv_sem=core_recv.at[u, origin],
            device_id={"shard": sibling},
            device_id_type=MESH,
        )

    for m, part in enumerate((a, b, c)):
        def begin(r, carry, m=m, part=part):
            u = m * cuts + r
            src = part.at[pl.ds(r * rows, rows)]

            @pl.when(chip < line - 1)
            def _():
                send(src, u, chip, 1).start()

            @pl.when(chip > 0)
            def _():
                send(src, u, chip, -1).start()

            share(src, u, chip).start()
            pltpu.make_async_copy(src, block(u, me), own_sem.at[u]).start()
            return carry

        lax.fori_loop(0, cuts, begin, 0)

    for step in range(1, line):
        def relay(u, carry, step=step):
            @pl.when(chip - step >= 0)
            def _():
                origin = chip - step
                got = block(u, 2 * origin + core)
                send(got, u, origin, 1).wait_recv()

                @pl.when(chip < line - 1)
                def _():
                    send(got, u, origin, 1).start()

                share(got, u, origin).start()

            @pl.when(chip + step < line)
            def _():
                origin = chip + step
                got = block(u, 2 * origin + core)
                send(got, u, origin, -1).wait_recv()

                @pl.when(chip > 0)
                def _():
                    send(got, u, origin, -1).start()

                share(got, u, origin).start()
            return carry

        lax.fori_loop(0, units, relay, 0)

    def finish(u, carry):
        pltpu.make_async_copy(a.at[pl.ds(0, rows)], block(u, me), own_sem.at[u]).wait()
        for d in range(line):
            got = block(u, 2 * d + core)
            share(got, u, d).wait()

            @pl.when(jnp.logical_and(d <= chip, chip < line - 1))
            def _(d=d, got=got):
                send(got, u, d, 1).wait_send()

            @pl.when(jnp.logical_and(d >= chip, chip > 0))
            def _(d=d, got=got):
                send(got, u, d, -1).wait_send()
        return carry

    lax.fori_loop(0, units, finish, 0)


def gather_all(shards, parts):
    rows_all, width = parts[0].shape
    line = shards // 2
    units = 3 * ROW_CUTS
    dma = pltpu.SemaphoreType.DMA
    return pl.pallas_call(
        functools.partial(gather_kernel, shards, ROW_CUTS),
        out_shape=jax.ShapeDtypeStruct((3 * rows_all, shards * width), jnp.bfloat16),
        in_specs=[pl.BlockSpec(memory_space=pl.ANY)] * 3,
        out_specs=pl.BlockSpec(memory_space=pl.ANY),
        scratch_shapes=[
            dma((units,)),
            dma((units, line)),
            dma((units, line)),
            dma((units, line)),
            dma((units, line)),
            dma((units, line)),
        ],
        compiler_params=pltpu.CompilerParams(
            collective_id=1, has_side_effects=True, vmem_limit_bytes=VMEM_BUDGET
        ),
        cost_estimate=pl.CostEstimate(
            flops=100_000_000_000, bytes_accessed=500_000_000, transcendentals=0
        ),
    )(*parts)


def use_kernels(shards, rows, cols):
    line = shards // 2
    chunk = 3 * rows * (cols // shards)
    need = chunk * (2 * (3 * line + 1) + 4)
    return shards % 2 == 0 and shards > 2 and need < VMEM_BUDGET - 8 * 1024 * 1024


def to_hidden_slices(parts):
    shards = lax.axis_size("shard")
    if use_kernels(shards, *parts[0].shape):
        return scatter_sum(shards, parts)
    return tuple(
        lax.psum_scatter(part, "shard", scatter_dimension=1, tiled=True).astype(jnp.float32)
        for part in parts
    )


def to_all_hidden(slices):
    shards = lax.axis_size("shard")
    rows, width = slices[0].shape
    if use_kernels(shards, rows, width * shards):
        full = gather_all(shards, slices)
        return full[:rows], full[rows : 2 * rows], full[2 * rows :]
    return tuple(lax.all_gather(part, "shard", axis=1, tiled=True) for part in slices)


def send_home(rows):
    experts = lax.axis_size("expert")
    shaped = rows.reshape(experts, rows.shape[0] // experts, rows.shape[1])
    return lax.all_to_all(shaped, "expert", split_axis=0, concat_axis=0, tiled=True)


def local(tokens, routes, mix_weights, cotangent, w_gate, w_up, w_down):
    experts = lax.axis_size("expert")
    expert = lax.axis_index("expert")
    w_gate, w_up, w_down = w_gate[0], w_up[0], w_down[0]

    routes_all = lax.all_gather(routes, "expert", axis=0, tiled=True)
    mix_all = lax.all_gather(mix_weights, "expert", axis=0, tiled=True)
    row_weight = jnp.sum(jnp.where(routes_all == expert, mix_all, 0.0), axis=1)[:, None]
    home_weight = jnp.sum(
        jnp.where(
            routes[None, :, :] == jnp.arange(experts, dtype=routes.dtype)[:, None, None],
            mix_weights[None, :, :],
            0.0,
        ),
        axis=2,
    )

    x_part = lax.all_gather(tokens, "expert", axis=0, tiled=True)
    cot_part = lax.all_gather(cotangent, "expert", axis=0, tiled=True)
    dy_part = (row_weight * cot_part.astype(jnp.float32)).astype(jnp.bfloat16)

    def partial(rows, weights):
        return jnp.dot(rows, weights, preferred_element_type=jnp.float32).astype(jnp.bfloat16)

    gate_pre, up_pre, d_hidden = to_hidden_slices(
        (partial(x_part, w_gate), partial(x_part, w_up), partial(dy_part, w_down))
    )

    sigmoid_gate = jax.nn.sigmoid(gate_pre)
    active = gate_pre * sigmoid_gate
    hidden = (active * up_pre).astype(jnp.bfloat16)
    d_gate = (d_hidden * up_pre * sigmoid_gate * (1.0 + gate_pre * (1.0 - sigmoid_gate))).astype(
        jnp.bfloat16
    )
    d_up = (d_hidden * active).astype(jnp.bfloat16)

    hidden_all, d_gate_all, d_up_all = to_all_hidden((hidden, d_gate, d_up))
    col_contract = (((1,), (1,)), ((), ()))
    out_rows = lax.dot_general(
        hidden_all, w_down, col_contract, preferred_element_type=jnp.float32
    ).astype(jnp.bfloat16)
    dx_rows = lax.dot_general(d_gate_all, w_gate, col_contract, preferred_element_type=jnp.float32)
    dx_rows = dx_rows + lax.dot_general(
        d_up_all, w_up, col_contract, preferred_element_type=jnp.float32
    )
    dx_rows = dx_rows.astype(jnp.bfloat16)
    out_home = send_home(out_rows)
    dx_home = send_home(dx_rows)
    layer_out = jnp.sum(home_weight[:, :, None] * out_home.astype(jnp.float32), axis=0).astype(
        jnp.bfloat16
    )
    grad_tokens = jnp.sum(dx_home.astype(jnp.float32), axis=0).astype(jnp.bfloat16)

    x_rows = lax.all_gather(
        lax.all_gather(tokens, "shard", axis=1, tiled=True), "expert", axis=0, tiled=True
    )
    cot_rows = lax.all_gather(
        lax.all_gather(cotangent, "shard", axis=1, tiled=True), "expert", axis=0, tiled=True
    )
    dy_rows = (row_weight * cot_rows.astype(jnp.float32)).astype(jnp.bfloat16)
    row_contract = (((0,), (0,)), ((), ()))

    def gradient(rows, slices):
        return lax.dot_general(
            rows, slices, row_contract, preferred_element_type=jnp.float32
        ).astype(jnp.bfloat16)

    grad_down = gradient(dy_rows, hidden)
    grad_gate = gradient(x_rows, d_gate)
    grad_up = gradient(x_rows, d_up)
    return (layer_out, grad_tokens, grad_gate[None], grad_up[None], grad_down[None])


def solution(mesh):
    return jax.shard_map(
        local,
        mesh=mesh,
        in_specs=(
            P("expert", "shard"),
            P("expert", None),
            P("expert", None),
            P("expert", "shard"),
            P("expert", "shard", None),
            P("expert", "shard", None),
            P("expert", "shard", None),
        ),
        out_specs=(
            P("expert", "shard"),
            P("expert", "shard"),
            P("expert", None, "shard"),
            P("expert", None, "shard"),
            P("expert", None, "shard"),
        ),
        check_vma=False,
    )
```

time: 809 us -> 494 us (0.61); the launches traced: 798 us -> 494 us
  waiting for transfers between devices: 348 us -> 8.93 us
  Pallas kernels: 0 us -> 333 us
  local copies, waits for them, and re-layouts: 202 us -> 20.3 us
  other arithmetic: 131 us -> 3.98 us
  blocking collectives: 0 us -> 37.3 us
  starting transfers between devices: 31.3 us -> 7.76 us
    pallas_call x0 -> x2, Pallas kernels: none -> 333 us  [the longest x1 167 us: gather_all(): pl.pallas_call(functools.partial(gather_kernel, shards, ROW_CUTS), out_sh...]
    all_to_all x5 -> x0, waiting for transfers between devices: 275 us -> none  [the longest x1 114 us: local(): lax.all_to_all(w_down, 'shard', split_axis=2, concat_axis=1, tiled=True)]
    unnamed x35 -> x24, local copies, waits for them, and re-layouts: 172 us -> 17.4 us
    unnamed x5 -> x2, other arithmetic: 125 us -> 0.01 us
    reduce_scatter x2 -> x0, waiting for transfers between devices: 71.4 us -> none  [feature_total(): lax.psum_scatter(partial_value.astype(jnp.bfloat16), 'shard', scatter_dim...]
    all_gather x0 -> x4, blocking collectives: none -> 37.3 us  [the longest x1 11.8 us: local(): cot_part = lax.all_gather(cotangent, 'expert', axis=0, tiled=True)]
    all_to_all x3 -> x0, local copies, waits for them, and re-layouts: 26.2 us -> none  [the longest x1 8.91 us: local(): lax.all_to_all(w_down, 'shard', split_axis=2, concat_axis=1, tiled=True)]
    all_to_all x5 -> x0, starting transfers between devices: 23.1 us -> none  [the longest x1 5.15 us: local(): lax.all_to_all(grad_send, 'expert', split_axis=0, concat_axis=0, tiled=True)]
  transfers between devices with their start and end apart: 11 -> 6, of which waited for: 6 -> 1; matrix products, arithmetic and copies ran while one was open for 47% -> 17% of each run, Pallas kernels for 0% -> 67%
where the time goes in v1:
time: 494 us
  Pallas kernels  333 us (67%)
  matrix products  68.9 us (14%)
  blocking collectives  37.3 us (8%)
  local copies, waits for them, and re-layouts  20.3 us (4%)
  between operations  13.9 us (3%)
  waiting for transfers between devices  8.93 us (2%)
  starting transfers between devices  7.76 us (2%)
    pallas_call x1, Pallas kernels, gather_all(): pl.pallas_call(functools.partial(gather_kernel, shards, ROW_CUTS), out_sh...  167 us
    pallas_call x1, Pallas kernels, scatter_sum(): pl.pallas_call(functools.partial(scatter_sum_kernel, shards, ROW_CUTS), o...  165 us
    dot_general x3, matrix products, gradient(): lax.dot_general(rows, slices, row_contract, preferred_element_type=jnp.fl...  23.6 us
    dot_general x3, matrix products, partial(): jnp.dot(rows, weights, preferred_element_type=jnp.float32)  22 us
    unnamed x24, local copies, waits for them, and re-layouts  17.4 us
    all_gather x1, blocking collectives, local(): cot_part = lax.all_gather(cotangent, 'expert', axis=0, tiled=True)  11.8 us
    all_gather x1, blocking collectives, local(): x_part = lax.all_gather(tokens, 'expert', axis=0, tiled=True)  10.4 us
  transfers between devices with their start and end apart: 6, of which 1 were waited for; matrix products, arithmetic and copies ran while one was open for 17% of the time, Pallas kernels for 67%

profile of v1, /device:TPU:0, one launch (start us, length us, event | category | flops | bytes accessed | tf_op | source)
XLA Modules:
  0.0 493.6 jit_solution(18160996249008607020)
XLA Ops:
  7.2 0.0 all-gather.5.cloned.1.call-start
  7.2 0.7 all-gather.5.cloned.1.call-update
  7.9 0.0 all-gather.9.cloned.1.call-start
  7.9 0.7 all-gather.9.cloned.1.call-update
  8.6 0.0 all-gather.7.cloned.1.call-start
  8.7 11.8 %all_gather.27 = bf16[512,512]{1,0:T(8,128)(2,1)S(1)} all-gather(bf16[128,512]{1,0:T(8,128)(2,1)} %param.10), channel_id=1, replica_groups=mesh['expert'=4,'shard'=8] {'expert'}, dimensions={0}, use_global_device_ids=true | all-gather | bytes 655360 | tf_op jit(solution)/shard_map/all_gather | solution.py:350
  20.5 10.4 %all_gather.24 = bf16[512,512]{1,0:T(8,128)(2,1)S(1)} all-gather(bf16[128,512]{1,0:T(8,128)(2,1)} %param.7), channel_id=1, replica_groups=mesh['expert'=4,'shard'=8] {'expert'}, dimensions={0}, use_global_device_ids=true | all-gather | bytes 655360 | tf_op jit(solution)/shard_map/all_gather | solution.py:349
  30.9 7.2 %all_gather.25 = s32[512,2]{0,1:T(2,128)S(1)} all-gather(s32[128,2]{0,1:T(2,128)} %param.8), channel_id=1, replica_groups=mesh['expert'=4,'shard'=8] {'expert'}, dimensions={0}, use_global_device_ids=true | all-gather | bytes 5120 | tf_op jit(solution)/shard_map/all_gather | solution.py:337
  38.1 7.9 %all_gather.26 = f32[512,2]{0,1:T(2,128)S(1)} all-gather(f32[128,2]{0,1:T(2,128)} %param.9), channel_id=1, replica_groups=mesh['expert'=4,'shard'=8] {'expert'}, dimensions={0}, use_global_device_ids=true | all-gather | bytes 5120 | tf_op jit(solution)/shard_map/all_gather | solution.py:338
  46.0 0.0 slice-start.2
  46.0 8.3 %convolution_convert_fusion.1.p1 = bf16[512,6144]{1,0:T(8,128)(2,1)} fusion(bf16[512,512]{1,0:T(8,128)(2,1)S(1)} %all_gather.24, bf16[1,512,6144]{2,1,0:T(8,128)(2,1)} %param.12), kind=kOutput, calls=%fused_computation.1 | convolution fusion | flops 3224371200 | bytes 13107200 | tf_op jit(solution)/shard_map/dot_general | solution.py:354
  54.3 0.0 slice-start.3
  54.3 0.0 copy-start.5
  54.3 8.3 %convolution_convert_fusion.2.p0 = bf16[512,6144]{1,0:T(8,128)(2,1)} fusion(bf16[512,512]{1,0:T(8,128)(2,1)S(1)} %all_gather.24, bf16[1,512,6144]{2,1,0:T(8,128)(2,1)} %param.11), kind=kOutput, calls=%fused_computation.2 | convolution fusion | flops 3224371200 | bytes 13107200 | tf_op jit(solution)/shard_map/dot_general | solution.py:354
  62.6 0.0 copy-done.5
  62.6 0.0 slice-done.2
  62.6 0.0 slice-done.3
  62.6 5.4 %convolution_convert_fusion.p2 = bf16[512,6144]{1,0:T(8,128)(2,1)} fusion(bf16[1,512,6144]{2,1,0:T(8,128)(2,1)S(1)} %bitcast.81, bf16[512,512]{1,0:T(8,128)(2,1)S(1)} %all_gather.27, f32[512]{0:T(512)S(1)} %fusion.41), kind=kOutput, calls=%fused_computation | convolution fusion | flops 3225157632 | bytes 13109248 | tf_op jit(solution)/shard_map/dot_general | solution.py:354
  68.0 0.0 all-gather.5.cloned.1.call-done
  68.0 0.0 all-gather.7.cloned.1.call-update
  68.1 0.0 all-gather.11.cloned.1.call-start
  68.1 165.1 %shard_map.110 = f32[6,256,768]{2,1,0:T(8,128)} custom-call(bf16[512,6144]{1,0:T(8,128)(2,1)} %convolution_convert_fusion.2.p0, bf16[512,6144]{1,0:T(8,128)(2,1)} %convolution_convert_fusion.1.p1, bf16[512,6144]{1,0:T(8,128)(2,1)} %convolution_convert_fusion.p2), custom_call_target="tpu_custom_call" | custom-call | flops 99999997952 | bytes 500000000 | tf_op jit(solution)/shard_map/pallas_call | solution.py:148
  233.2 2.9 fusion.42
  236.1 0.0 slice-start
  236.1 2.4 fusion.19
  238.5 0.0 all-gather.9.cloned.1.call-done
  238.5 0.0 all-gather.11.cloned.1.call-update
  238.5 0.0 slice-start.1
  238.5 167.5 %shard_map.111 = bf16[1536,6144]{1,0:T(8,128)(2,1)} custom-call(bf16[512,768]{1,0:T(8,128)(2,1)} %get-tuple-element.20.a, bf16[512,768]{1,0:T(8,128)(2,1)} %get-tuple-element.19.b, bf16[512,768]{1,0:T(8,128)(2,1)} %get-tuple-element.18.c), custom_call_target="tpu_custom_call" | custom-call | flops 99999997952 | bytes 500000000 | tf_op jit(solution)/shard_map/pallas_call | solution.py:278
  406.0 0.0 slice-done
  406.0 0.0 slice-done.1
  406.0 5.6 %fusion.3 = f32[512,512]{1,0:T(8,128)S(1)} fusion(bf16[1,512,6144]{2,1,0:T(8,128)(2,1)S(1)} %bitcast.79, bf16[1536,6144]{1,0:T(8,128)(2,1)} %shard_map.111), kind=kOutput, calls=%fused_computation.10 | convolution fusion | flops 3221225472 | bytes 13631488 | tf_op jit(solution)/shard_map/dot_general | solution.py:374
  411.6 8.8 %fusion.30 = bf16[512,512]{1,0:T(8,128)(2,1)} fusion(f32[512,512]{1,0:T(8,128)S(1)} %fusion.3, bf16[1,512,6144]{2,1,0:T(8,128)(2,1)} %param.11, bf16[1536,6144]{1,0:T(8,128)(2,1)} %shard_map.111), kind=kOutput, calls=%fused_computation.39 | convolution fusion | flops 3221749760 | bytes 14155776 | tf_op jit(solution)/shard_map/dot_general | solution.py:373
  420.4 3.5 all-to-all-start.1
  423.9 0.0 copy-start.3
  423.9 0.0 copy-start.4
  423.9 0.0 copy-start.2
  424.0 8.9 %fusion.35 = bf16[512,512]{1,0:T(8,128)(2,1)} fusion(bf16[1,512,6144]{2,1,0:T(8,128)(2,1)} %param.13, bf16[1536,6144]{1,0:T(8,128)(2,1)} %shard_map.111), kind=kOutput, calls=%fused_computation.40 | convolution fusion | flops 3221487616 | bytes 13107200 | tf_op jit(solution)/shard_map/dot_general | solution.py:370
  432.9 0.0 all-to-all-done.1
  432.9 4.1 all-to-all-start
  437.0 0.0 copy-done.3
  437.0 0.0 copy-done.4
  437.0 0.7 reduce_sum.42
  437.8 7.5 %all-to-all-done = bf16[4,128,512]{2,1,0:T(8,128)(2,1)S(1)} async-done(((bf16[4,128,512]{2,1,0:T(8,128)(2,1)}), bf16[4,128,512]{2,1,0:T(8,128)(2,1)S(1)}, u32[]{:S(2)}, u32[]{:S(2)}) %all-to-all-start) | async-done | bytes 524320 | tf_op jit(solution)/shard_map/all_to_all | solution.py:329
  445.3 0.8 multiply_reduce_fusion
  446.1 0.0 all-gather.7.cloned.1.call-done
  446.1 0.0 copy-done.2
  446.1 7.5 %fusion.12 = bf16[1,4096,768]{1,2,0:T(8,128)(2,1)} fusion(bf16[512,768]{1,0:T(8,128)(2,1)S(1)} %copy-done.2, bf16[512,4096]{1,0:T(8,128)(2,1)} %all-gather.7.cloned.1.call-done), kind=kOutput, calls=%fused_computation.19 | convolution fusion | flops 3224371200 | bytes 11272192 | tf_op jit(solution)/shard_map/dot_general | solution.py:395
  453.7 0.0 copy-start.1
  453.7 8.7 %copy.16 = bf16[1,4096,768]{2,1,0:T(8,128)(2,1)} copy(bf16[1,4096,768]{1,2,0:T(8,128)(2,1)} %fusion.12) | data formatting | bytes 12582912
  462.4 0.0 copy-done.1
  462.4 7.5 %fusion.13 = bf16[1,4096,768]{1,2,0:T(8,128)(2,1)} fusion(bf16[512,768]{1,0:T(8,128)(2,1)S(1)} %copy-done.1, bf16[512,4096]{1,0:T(8,128)(2,1)} %all-gather.7.cloned.1.call-done), kind=kOutput, calls=%fused_computation.20 | convolution fusion | flops 3224371200 | bytes 11272192 | tf_op jit(solution)/shard_map/dot_general | solution.py:395
  469.9 0.0 copy-start
  469.9 0.0 copy-start.6
  469.9 8.7 %copy.17 = bf16[1,4096,768]{2,1,0:T(8,128)(2,1)} copy(bf16[1,4096,768]{1,2,0:T(8,128)(2,1)} %fusion.13) | data formatting | bytes 12582912
  478.6 0.0 all-gather.11.cloned.1.call-done
  478.6 0.0 copy-done
  478.6 0.0 copy-done.6
  478.6 8.5 %fusion.14 = bf16[1,4096,768]{2,1,0:T(8,128)(2,1)} fusion(bf16[512,768]{1,0:T(8,128)(2,1)S(1)} %copy-done, bf16[512,4096]{1,0:T(8,128)(2,1)} %all-gather.11.cloned.1.call-done, f32[512]{0:T(512)S(1)} %copy-done.6), kind=kOutput, calls=%fused_computation.21 | convolution fusion | flops 3230662656 | bytes 11274240 | tf_op jit(solution)/shard_map/dot_general | solution.py:395
  (4 shorter events, 0.0 us)
Async XLA Ops:
  7.2 60.9 %all-gather.5.cloned.1.call-start = ((), (), s32[]{:S(2)}) async-start(), calls=%async_computation.2 | async-start | bytes 1179648 | tf_op jit(solution)/shard_map/all_gather | solution.py:386
  7.9 230.6 %all-gather.9.cloned.1.call-start = ((), (), s32[]{:S(2)}) async-start(), calls=%async_computation.4 | async-start | bytes 1179648 | tf_op jit(solution)/shard_map/all_gather | solution.py:389
  8.6 437.5 %all-gather.7.cloned.1.call-start = ((), (), s32[]{:S(2)}) async-start(), calls=%async_computation.3 | async-start | bytes 5242880 | tf_op jit(solution)/shard_map/all_gather | solution.py:385
  46.0 16.6 %slice-start.2 = ((s8[6291456]{0:T(1024)(128)(4,1)}), s8[4194304]{0:T(1024)(128)(4,1)S(1)}, s32[]{:S(2)}) async-start(s8[6291456]{0:T(1024)(128)(4,1)} %bitcast.80), calls=%async_computation.8 | async-start | bytes 8388608
  54.3 8.3 %slice-start.3 = ((s8[6291456]{0:T(1024)(128)(4,1)}), s8[2097152]{0:T(1024)(128)(4,1)S(1)}, s32[]{:S(2)}) async-start(s8[6291456]{0:T(1024)(128)(4,1)} %bitcast.80), calls=%async_computation.9 | async-start | bytes 4194304
  54.3 8.3 %copy-start.5 = (f32[512]{0:T(512)}, f32[512]{0:T(512)S(1)}, u32[]{:S(2)}) copy-start(f32[512]{0:T(512)S(1)} %fusion.41) | copy-start | bytes 6148
  68.1 410.5 %all-gather.11.cloned.1.call-start = ((), (), s32[]{:S(2)}) async-start(), calls=%async_computation.5 | async-start | bytes 5242880 | tf_op jit(solution)/shard_map/all_gather | solution.py:388
  236.1 169.9 %slice-start = ((s8[6291456]{0:T(1024)(128)(4,1)}), s8[2097152]{0:T(1024)(128)(4,1)S(1)}, s32[]{:S(2)}) async-start(s8[6291456]{0:T(1024)(128)(4,1)} %bitcast.78), calls=%async_computation.6 | async-start | bytes 4194304
  238.5 167.5 %slice-start.1 = ((s8[6291456]{0:T(1024)(128)(4,1)}), s8[4194304]{0:T(1024)(128)(4,1)S(1)}, s32[]{:S(2)}) async-start(s8[6291456]{0:T(1024)(128)(4,1)} %bitcast.78), calls=%async_computation.7 | async-start | bytes 8388608
  420.4 12.4 %all-to-all-start.1 = ((bf16[4,128,512]{2,1,0:T(8,128)(2,1)}), bf16[4,128,512]{2,1,0:T(8,128)(2,1)S(1)}, u32[]{:S(2)}, u32[]{:S(2)}) async-start(bf16[4,128,512]{2,1,0:T(8,128)(2,1)} %bitcast.7), calls=%async_computation.1 | async-start | bytes 1048576 | tf_op jit(solution)/shard_map/all_to_all | solution.py:329
  423.9 13.1 %copy-start.3 = (f32[128,2]{0,1:T(2,128)S(1)}, f32[128,2]{0,1:T(2,128)}, u32[]{:S(2)}) copy-start(f32[128,2]{0,1:T(2,128)} %param.9) | copy-start | bytes 3076
  423.9 13.1 %copy-start.4 = (s32[128,2]{0,1:T(2,128)S(1)}, s32[128,2]{0,1:T(2,128)}, u32[]{:S(2)}) copy-start(s32[128,2]{0,1:T(2,128)} %param.8) | copy-start | bytes 3076
  423.9 22.2 %copy-start.2 = (bf16[512,768]{1,0:T(8,128)(2,1)S(1)}, bf16[512,768]{1,0:T(8,128)(2,1)}, u32[]{:S(2)}) copy-start(bf16[512,768]{1,0:T(8,128)(2,1)} %get-tuple-element.19.b) | copy-start | bytes 2359300
  432.9 12.4 %all-to-all-start = ((bf16[4,128,512]{2,1,0:T(8,128)(2,1)}), bf16[4,128,512]{2,1,0:T(8,128)(2,1)S(1)}, u32[]{:S(2)}, u32[]{:S(2)}) async-start(bf16[4,128,512]{2,1,0:T(8,128)(2,1)} %bitcast.6), calls=%async_computation | async-start | bytes 1048576 | tf_op jit(solution)/shard_map/all_to_all | solution.py:329
  453.7 8.7 %copy-start.1 = (bf16[512,768]{1,0:T(8,128)(2,1)S(1)}, bf16[512,768]{1,0:T(8,128)(2,1)}, u32[]{:S(2)}) copy-start(bf16[512,768]{1,0:T(8,128)(2,1)} %get-tuple-element.18.c) | copy-start | bytes 2359300
  469.9 8.7 %copy-start = (bf16[512,768]{1,0:T(8,128)(2,1)S(1)}, bf16[512,768]{1,0:T(8,128)(2,1)}, u32[]{:S(2)}) copy-start(bf16[512,768]{1,0:T(8,128)(2,1)} %get-tuple-element.20.a) | copy-start | bytes 2359300
  469.9 8.7 %copy-start.6 = (f32[512]{0:T(512)S(1)}, f32[512]{0:T(512)}, u32[]{:S(2)}) copy-start(f32[512]{0:T(512)} %copy-done.5) | copy-start | bytes 6148
Sparse Core Ops, SparseCore 0:
  9.6 24.7 all-gather.4
  36.0 21.7 all-gather.8
  68.2 52.8 all-gather.6
  238.6 61.2 all-gather.10

commit v2 on v0

v2 whole, which is shorter than its diff:
```python
import functools

import jax
import jax.numpy as jnp
from jax import lax
from jax.experimental import pallas as pl
from jax.experimental.pallas import tpu as pltpu
from jax.sharding import PartitionSpec as P

MESH = pl.DeviceIdType.MESH
VMEM_BUDGET = 56 * 1024 * 1024
BLOCKS = 8


def place(shards):
    me = lax.axis_index("shard")
    chip = me // 2
    core = me % 2
    return me, chip, core, me + 1 - 2 * core


def greet(me, chip, sibling, line):
    barrier = pltpu.get_barrier_semaphore()
    pl.semaphore_signal(barrier, inc=1, device_id={"shard": sibling}, device_id_type=MESH)

    @pl.when(chip > 0)
    def _():
        pl.semaphore_signal(barrier, inc=1, device_id={"shard": me - 2}, device_id_type=MESH)

    @pl.when(chip < line - 1)
    def _():
        pl.semaphore_signal(barrier, inc=1, device_id={"shard": me + 2}, device_id_type=MESH)

    peers = jnp.where(chip > 0, 2, 1) + jnp.where(chip < line - 1, 1, 0)
    pl.semaphore_wait(barrier, peers)


def exchange_kernel(
    shards, blocks, p0, p1, p2, mine, full, stage, core_in, line_in,
    load_sem, core_send, core_recv, line_send, line_recv,
    ring_right, ring_left, ring_recv, pair_send, pair_recv, own_sem,
):
    line = shards // 2
    rows, width = stage.shape[3], stage.shape[4]
    me, chip, core, sibling = place(shards)
    left_half = 2 * chip < line
    greet(me, chip, sibling, line)

    def rows_of(r):
        return pl.ds(pl.multiple_of(r * rows, rows), rows)

    def cols_of(shard):
        return pl.ds(pl.multiple_of(shard * width, 128), width)

    def turn(j):
        return jnp.where(left_half, line - 1 - j, j)

    def load(part, r, d, m):
        return pltpu.make_async_copy(
            part.at[rows_of(r), cols_of(2 * d + core)], stage.at[r, d, m], load_sem.at[r, d, m]
        )

    def swap(part, r, d, m):
        return pltpu.make_async_remote_copy(
            src_ref=part.at[rows_of(r), cols_of(2 * d + 1 - core)],
            dst_ref=core_in.at[r, d, m],
            send_sem=core_send.at[r, d, m],
            recv_sem=core_recv.at[r, d, m],
            device_id={"shard": sibling},
            device_id_type=MESH,
        )

    def pass_on(r, d, slot, to):
        return pltpu.make_async_remote_copy(
            src_ref=stage.at[r, d],
            dst_ref=line_in.at[r, slot],
            send_sem=line_send.at[r, d],
            recv_sem=line_recv.at[r, slot],
            device_id={"shard": to},
            device_id_type=MESH,
        )

    def block(r, shard):
        return full.at[:, rows_of(r), cols_of(shard)]

    def send(src, r, origin, way):
        return pltpu.make_async_remote_copy(
            src_ref=src,
            dst_ref=block(r, 2 * origin + core),
            send_sem=(ring_right if way > 0 else ring_left).at[r, origin],
            recv_sem=ring_recv.at[r, origin],
            device_id={"shard": me + 2 * way},
            device_id_type=MESH,
        )

    def share(src, r, origin):
        return pltpu.make_async_remote_copy(
            src_ref=src,
            dst_ref=block(r, 2 * origin + core),
            send_sem=pair_send.at[r, origin],
            recv_sem=pair_recv.at[r, origin],
            device_id={"shard": sibling},
            device_id_type=MESH,
        )

    def keep(r):
        return pltpu.make_async_copy(mine.at[:, rows_of(r)], block(r, me), own_sem.at[r])

    def wide(value):
        return value.astype(jnp.float32)

    def begin(r):
        for j in range(line):
            for m, part in enumerate((p0, p1, p2)):
                swap(part, r, turn(j), m).start()
                load(part, r, turn(j), m).start()

    def arrived(r, d):
        for m in range(3):
            load(p0, r, d, m).wait()
            swap(p0, r, d, m).wait_recv()

    def relay(r):
        for j in range(line):
            d = turn(j)

            @pl.when(chip != d)
            def _(d=d):
                rightward = chip < d
                slot = jnp.where(rightward, d + 1, d)
                to = jnp.where(rightward, me + 2, me - 2)
                at_end = jnp.where(rightward, chip, line - 1 - chip) == 0
                arrived(r, d)

                @pl.when(at_end)
                def _():
                    for m in range(3):
                        stage[r, d, m] = (wide(stage[r, d, m]) + wide(core_in[r, d, m])).astype(
                            stage.dtype
                        )

                @pl.when(jnp.logical_not(at_end))
                def _():
                    pass_on(r, d, slot, to).wait_recv()
                    for m in range(3):
                        stage[r, d, m] = (
                            wide(stage[r, d, m]) + wide(core_in[r, d, m]) + wide(line_in[r, slot, m])
                        ).astype(stage.dtype)

                pass_on(r, d, slot, to).start()

    def finish(r):
        arrived(r, chip)

        def total(m):
            return wide(stage[r, chip, m]) + wide(core_in[r, chip, m])

        def store(gate_pre, up_pre, d_hidden):
            sigmoid_gate = jax.nn.sigmoid(gate_pre)
            active = gate_pre * sigmoid_gate
            slope = sigmoid_gate * (1.0 + gate_pre * (1.0 - sigmoid_gate))
            mine[0, rows_of(r)] = (active * up_pre).astype(mine.dtype)
            mine[1, rows_of(r)] = (d_hidden * up_pre * slope).astype(mine.dtype)
            mine[2, rows_of(r)] = (d_hidden * active).astype(mine.dtype)

        @pl.when(chip == 0)
        def _():
            pass_on(r, chip, chip, sibling).wait_recv()
            store(*[total(m) + wide(line_in[r, chip, m]) for m in range(3)])

        @pl.when(chip == line - 1)
        def _():
            pass_on(r, chip, chip + 1, sibling).wait_recv()
            store(*[total(m) + wide(line_in[r, chip + 1, m]) for m in range(3)])

        @pl.when(jnp.logical_and(chip > 0, chip < line - 1))
        def _():
            pass_on(r, chip, chip, sibling).wait_recv()
            pass_on(r, chip, chip + 1, sibling).wait_recv()
            store(
                *[
                    total(m) + wide(line_in[r, chip, m]) + wide(line_in[r, chip + 1, m])
                    for m in range(3)
                ]
            )

        src = mine.at[:, rows_of(r)]

        @pl.when(chip < line - 1)
        def _():
            send(src, r, chip, 1).start()

        @pl.when(chip > 0)
        def _():
            send(src, r, chip, -1).start()

        share(src, r, chip).start()
        keep(r).start()

    def forward(r, step):
        @pl.when(chip - step >= 0)
        def _():
            origin = chip - step
            got = block(r, 2 * origin + core)
            send(got, r, origin, 1).wait_recv()

            @pl.when(chip < line - 1)
            def _():
                send(got, r, origin, 1).start()

            share(got, r, origin).start()

        @pl.when(chip + step < line)
        def _():
            origin = chip + step
            got = block(r, 2 * origin + core)
            send(got, r, origin, -1).wait_recv()

            @pl.when(chip > 0)
            def _():
                send(got, r, origin, -1).start()

            share(got, r, origin).start()

    begin(0)

    def advance(i, carry):
        @pl.when(i + 1 < blocks)
        def _():
            begin(i + 1)

        @pl.when(i < blocks)
        def _():
            relay(i)

        @pl.when(jnp.logical_and(i >= 1, i - 1 < blocks))
        def _():
            finish(i - 1)

        for step in range(1, line):
            @pl.when(jnp.logical_and(i >= 1 + step, i - 1 - step < blocks))
            def _(step=step):
                forward(i - 1 - step, step)
        return carry

    lax.fori_loop(0, blocks + line, advance, 0)

    def settle(r, carry):
        keep(r).wait()
        for d in range(line):
            got = block(r, 2 * d + core)
            share(got, r, d).wait()
            for m in range(3):
                swap(p0, r, d, m).wait_send()

            @pl.when(chip != d)
            def _(d=d):
                pass_on(r, d, d, sibling).wait_send()

            @pl.when(jnp.logical_and(d <= chip, chip < line - 1))
            def _(d=d, got=got):
                send(got, r, d, 1).wait_send()

            @pl.when(jnp.logical_and(d >= chip, chip > 0))
            def _(d=d, got=got):
                send(got, r, d, -1).wait_send()
        return carry

    lax.fori_loop(0, blocks, settle, 0)


def exchange(shards, parts):
    rows_all, cols = parts[0].shape
    rows, width, line = rows_all // BLOCKS, cols // shards, shards // 2
    dma = pltpu.SemaphoreType.DMA
    pairs, triples = (BLOCKS, line), (BLOCKS, line, 3)
    chunks = (BLOCKS, line, 3, rows, width)
    return pl.pallas_call(
        functools.partial(exchange_kernel, shards, BLOCKS),
        out_shape=(
            jax.ShapeDtypeStruct((3, rows_all, width), jnp.bfloat16),
            jax.ShapeDtypeStruct((3, rows_all, cols), jnp.bfloat16),
        ),
        in_specs=[pl.BlockSpec(memory_space=pl.ANY)] * 3,
        out_specs=(pl.BlockSpec(memory_space=pltpu.VMEM), pl.BlockSpec(memory_space=pl.ANY)),
        scratch_shapes=[
            pltpu.VMEM(chunks, jnp.bfloat16),
            pltpu.VMEM(chunks, jnp.bfloat16),
            pltpu.VMEM((BLOCKS, line + 1, 3, rows, width), jnp.bfloat16),
            dma(triples),
            dma(triples),
            dma(triples),
            dma(pairs),
            dma((BLOCKS, line + 1)),
            dma(pairs),
            dma(pairs),
            dma(pairs),
            dma(pairs),
            dma(pairs),
            dma((BLOCKS,)),
        ],
        compiler_params=pltpu.CompilerParams(
            collective_id=0, has_side_effects=True, vmem_limit_bytes=VMEM_BUDGET
        ),
        cost_estimate=pl.CostEstimate(
            flops=200_000_000_000, bytes_accessed=800_000_000, transcendentals=0
        ),
    )(*parts)


def use_kernels(shards, rows, cols):
    line = shards // 2
    chunk = 3 * rows * (cols // shards)
    need = chunk * (2 * (3 * line + 1) + 4)
    return shards % 2 == 0 and shards > 2 and need < VMEM_BUDGET - 8 * 1024 * 1024


def activate(gate_pre, up_pre, d_hidden):
    sigmoid_gate = jax.nn.sigmoid(gate_pre)
    active = gate_pre * sigmoid_gate
    hidden = active * up_pre
    d_gate = d_hidden * up_pre * sigmoid_gate * (1.0 + gate_pre * (1.0 - sigmoid_gate))
    return tuple(value.astype(jnp.bfloat16) for value in (hidden, d_gate, d_hidden * active))


def to_hidden(parts):
    shards = lax.axis_size("shard")
    if use_kernels(shards, *parts[0].shape):
        return exchange(shards, parts)
    sums = [
        lax.psum_scatter(part, "shard", scatter_dimension=1, tiled=True).astype(jnp.float32)
        for part in parts
    ]
    mine = activate(*sums)
    return mine, tuple(lax.all_gather(part, "shard", axis=1, tiled=True) for part in mine)


def send_home(rows):
    experts = lax.axis_size("expert")
    shaped = rows.reshape(experts, rows.shape[0] // experts, rows.shape[1])
    return lax.all_to_all(shaped, "expert", split_axis=0, concat_axis=0, tiled=True)


def local(tokens, routes, mix_weights, cotangent, w_gate, w_up, w_down):
    experts = lax.axis_size("expert")
    w_gate, w_up, w_down = w_gate[0], w_up[0], w_down[0]

    home_weight = jnp.sum(
        jnp.where(
            routes[None, :, :] == jnp.arange(experts, dtype=routes.dtype)[:, None, None],
            mix_weights[None, :, :],
            0.0,
        ),
        axis=2,
    )
    features = tokens.shape[1]
    dy_home = (home_weight[:, :, None] * cotangent.astype(jnp.float32)[None]).astype(jnp.bfloat16)
    sent = jnp.concatenate([jnp.broadcast_to(tokens[None], dy_home.shape), dy_home], axis=2)
    got = lax.all_to_all(sent, "expert", split_axis=0, concat_axis=0, tiled=True)
    got = got.reshape(-1, 2 * features)
    x_part, dy_part = got[:, :features], got[:, features:]
    row_weight = lax.all_to_all(
        home_weight[:, None, :], "expert", split_axis=0, concat_axis=0, tiled=True
    ).reshape(-1, 1)

    def partial(rows, weights):
        return jnp.dot(rows, weights, preferred_element_type=jnp.float32).astype(jnp.bfloat16)

    (hidden, d_gate, d_up), (hidden_all, d_gate_all, d_up_all) = to_hidden(
        (partial(x_part, w_gate), partial(x_part, w_up), partial(dy_part, w_down))
    )
    col_contract = (((1,), (1,)), ((), ()))
    out_rows = lax.dot_general(
        hidden_all, w_down, col_contract, preferred_element_type=jnp.float32
    ).astype(jnp.bfloat16)
    dx_rows = lax.dot_general(d_gate_all, w_gate, col_contract, preferred_element_type=jnp.float32)
    dx_rows = dx_rows + lax.dot_general(
        d_up_all, w_up, col_contract, preferred_element_type=jnp.float32
    )
    dx_rows = dx_rows.astype(jnp.bfloat16)
    out_home = send_home(out_rows)
    dx_home = send_home(dx_rows)
    layer_out = jnp.sum(home_weight[:, :, None] * out_home.astype(jnp.float32), axis=0).astype(
        jnp.bfloat16
    )
    grad_tokens = jnp.sum(dx_home.astype(jnp.float32), axis=0).astype(jnp.bfloat16)

    x_rows = lax.all_gather(
        lax.all_gather(tokens, "shard", axis=1, tiled=True), "expert", axis=0, tiled=True
    )
    x_rows = jnp.where(row_weight > 0, x_rows, jnp.zeros_like(x_rows))
    cot_rows = lax.all_gather(
        lax.all_gather(cotangent, "shard", axis=1, tiled=True), "expert", axis=0, tiled=True
    )
    dy_rows = (row_weight * cot_rows.astype(jnp.float32)).astype(jnp.bfloat16)
    row_contract = (((0,), (0,)), ((), ()))

    def gradient(rows, slices):
        return lax.dot_general(
            rows, slices, row_contract, preferred_element_type=jnp.float32
        ).astype(jnp.bfloat16)

    grad_down = gradient(dy_rows, hidden)
    grad_gate = gradient(x_rows, d_gate)
    grad_up = gradient(x_rows, d_up)
    return (layer_out, grad_tokens, grad_gate[None], grad_up[None], grad_down[None])


def solution(mesh):
    return jax.shard_map(
        local,
        mesh=mesh,
        in_specs=(
            P("expert", "shard"),
            P("expert", None),
            P("expert", None),
            P("expert", "shard"),
            P("expert", "shard", None),
            P("expert", "shard", None),
            P("expert", "shard", None),
        ),
        out_specs=(
            P("expert", "shard"),
            P("expert", "shard"),
            P("expert", None, "shard"),
            P("expert", None, "shard"),
            P("expert", None, "shard"),
        ),
        check_vma=False,
    )
```

time: 809 us -> 414 us (0.51); the launches traced: 798 us -> 414 us
  waiting for transfers between devices: 348 us -> 33.8 us
  Pallas kernels: 0 us -> 263 us
  local copies, waits for them, and re-layouts: 202 us -> 0.97 us
  other arithmetic: 131 us -> 6.07 us
  starting transfers between devices: 31.3 us -> 11.8 us
  blocking collectives: 0 us -> 18 us
    all_to_all x5 -> x1, waiting for transfers between devices: 275 us -> 0.01 us  [local(): lax.all_to_all(home_weight[:, None, :], 'expert', split_axis=0, concat_ax...]
    pallas_call x0 -> x1, Pallas kernels: none -> 263 us  [exchange(): pl.pallas_call(functools.partial(exchange_kernel, shards, BLOCKS), out_sh...]
    unnamed x35 -> x12, local copies, waits for them, and re-layouts: 172 us -> 0.03 us
    unnamed x5 -> x1, other arithmetic: 125 us -> 0.01 us
    reduce_scatter x2 -> x0, waiting for transfers between devices: 71.4 us -> none  [feature_total(): lax.psum_scatter(partial_value.astype(jnp.bfloat16), 'shard', scatter_dim...]
    all_to_all x3 -> x0, local copies, waits for them, and re-layouts: 26.2 us -> none  [the longest x1 8.91 us: local(): lax.all_to_all(w_down, 'shard', split_axis=2, concat_axis=1, tiled=True)]
    all_gather x2 -> x4, waiting for transfers between devices: 0.02 us -> 25.7 us  [the longest x1 25.7 us: local(): lax.all_gather(tokens, 'shard', axis=1, tiled=True)]
    all_to_all x5 -> x1, starting transfers between devices: 23.1 us -> 3.77 us  [local(): lax.all_to_all(home_weight[:, None, :], 'expert', split_axis=0, concat_ax...]
  transfers between devices with their start and end apart: 11 -> 7, of which waited for: 6 -> 2; matrix products, arithmetic and copies ran while one was open for 47% -> 16% of each run, Pallas kernels for 0% -> 64%
where the time goes in v2:
time: 414 us
  Pallas kernels  263 us (64%)
  matrix products  66 us (16%)
  waiting for transfers between devices  33.8 us (8%)
  blocking collectives  18 us (4%)
  between operations  13.9 us (3%)
  starting transfers between devices  11.8 us (3%)
  other arithmetic  6.07 us (1%)
    pallas_call x1, Pallas kernels, exchange(): pl.pallas_call(functools.partial(exchange_kernel, shards, BLOCKS), out_sh...  263 us
    all_gather x1, waiting for transfers between devices, local(): lax.all_gather(tokens, 'shard', axis=1, tiled=True)  25.7 us
    dot_general x3, matrix products, gradient(): lax.dot_general(rows, slices, row_contract, preferred_element_type=jnp.fl...  22.7 us
    dot_general x3, matrix products, partial(): jnp.dot(rows, weights, preferred_element_type=jnp.float32)  21.8 us
    all_to_all x1, blocking collectives, local(): lax.all_to_all(sent, 'expert', split_axis=0, concat_axis=0, tiled=True)  18 us
    dot_general x1, matrix products, local(): lax.dot_general(hidden_all, w_down, col_contract, preferred_element_type=...  8.98 us
  transfers between devices with their start and end apart: 7, of which 2 were waited for; matrix products, arithmetic and copies ran while one was open for 16% of the time, Pallas kernels for 64%

profile of v2, /device:TPU:0, one launch (start us, length us, event | category | flops | bytes accessed | tf_op | source)
XLA Modules:
  0.0 413.7 jit_solution(12027368723822750491)
XLA Ops:
  7.2 0.0 all-gather.5.cloned.1.call-start
  7.2 0.7 all-gather.5.cloned.1.call-update
  7.9 0.0 all-gather.9.cloned.1.call-start
  7.9 0.7 all-gather.9.cloned.1.call-update
  8.6 0.0 all-gather.7.cloned.1.call-start
  8.7 25.7 %all-gather.5.cloned.1.call-done = bf16[128,4096]{1,0:T(8,128)(2,1)} async-done(((bf16[128,512]{1,0:T(8,128)(2,1)}), bf16[128,4096]{1,0:T(8,128)(2,1)}) %all-gather.5.cloned.1.call-update) | async-done | bytes 1048592 | tf_op jit(solution)/shard_map/all_gather | solution.py:389
  34.4 0.0 all-gather.7.cloned.1.call-update
  34.5 0.9 convert_element_type.44
  35.4 1.3 select_reduce_fusion
  36.7 0.8 multiply_convert_fusion.2
  37.5 0.9 broadcast_in_dim.49
  38.5 0.1 pad_maximum_fusion
  38.6 18.0 %all_to_all.20 = bf16[4,128,1024]{2,1,0:T(8,128)(2,1)S(1)} all-to-all(bf16[4,128,1024]{2,1,0:T(8,128)(2,1)S(1)} %pad_maximum_fusion), channel_id=1, replica_groups=mesh['expert'=4,'shard'=8] {'expert'}, dimensions={0} | all-to-all | bytes 2097152 | tf_op jit(solution)/shard_map/all_to_all | solution.py:359
  56.6 3.8 all-to-all-start.3
  60.3 0.0 all-gather.11.cloned.1.call-start
  60.4 0.0 slice-start
  60.4 8.2 %convolution_convert_fusion.2.p0 = bf16[512,6144]{1,0:T(8,128)(2,1)} fusion(bf16[1,512,6144]{2,1,0:T(8,128)(2,1)} %param.11, bf16[512,1024]{1,0:T(8,128)(2,1)S(1)} %bitcast.58), kind=kOutput, calls=%fused_computation.2 | convolution fusion | flops 3224371200 | bytes 13107200 | tf_op jit(solution)/shard_map/dot_general | solution.py:367
  68.6 0.0 slice-start.1
  68.6 8.2 %convolution_convert_fusion.1.p1 = bf16[512,6144]{1,0:T(8,128)(2,1)} fusion(bf16[1,512,6144]{2,1,0:T(8,128)(2,1)} %param.12, bf16[512,1024]{1,0:T(8,128)(2,1)S(1)} %bitcast.59), kind=kOutput, calls=%fused_computation.1 | convolution fusion | flops 3224371200 | bytes 13107200 | tf_op jit(solution)/shard_map/dot_general | solution.py:367
  76.9 0.0 slice-done
  76.9 0.0 slice-done.1
  76.9 5.4 %convolution_convert_fusion.p2 = bf16[512,6144]{1,0:T(8,128)(2,1)} fusion(bf16[1,512,6144]{2,1,0:T(8,128)(2,1)S(1)} %bitcast.62, bf16[512,1024]{1,0:T(8,128)(2,1)S(1)} %bitcast.60), kind=kOutput, calls=%fused_computation | convolution fusion | flops 3224371200 | bytes 13107200 | tf_op jit(solution)/shard_map/dot_general | solution.py:367
  82.2 0.0 all-gather.9.cloned.1.call-done
  82.2 0.0 all-gather.11.cloned.1.call-update
  82.3 0.0 copy-start
  82.3 263.1 %shard_map.110 = (bf16[3,512,768]{2,1,0:T(8,128)(2,1)}, bf16[3,512,6144]{2,1,0:T(8,128)(2,1)}) custom-call(bf16[512,6144]{1,0:T(8,128)(2,1)} %convolution_convert_fusion.2.p0, bf16[512,6144]{1,0:T(8,128)(2,1)} %convolution_convert_fusion.1.p1, bf16[512,6144]{1,0:T(8,128)(2,1)} %convolution_convert_fusion.p2), custom_call_target="tpu_custom_call" | custom-call | flops 199999995904 | bytes 800000000 | tf_op jit(solution)/shard_map/pallas_call | solution.py:278
  345.4 0.0 copy-done
  345.4 0.0 copy-start.1
  345.4 5.7 %fusion = f32[512,512]{1,0:T(8,128)S(1)} fusion(bf16[1,512,6144]{2,1,0:T(8,128)(2,1)S(1)} %copy-done, bf16[3,512,6144]{2,1,0:T(8,128)(2,1)} %get-tuple-element.7), kind=kOutput, calls=%fused_computation.7 | convolution fusion | flops 3221225472 | bytes 13631488 | tf_op jit(solution)/shard_map/dot_general | solution.py:377
  351.2 0.0 copy-done.1
  351.2 6.8 %fusion.24 = bf16[512,512]{1,0:T(8,128)(2,1)} fusion(f32[512,512]{1,0:T(8,128)S(1)} %fusion, bf16[1,512,6144]{2,1,0:T(8,128)(2,1)S(1)} %copy-done.1, bf16[3,512,6144]{2,1,0:T(8,128)(2,1)} %get-tuple-element.7), kind=kOutput, calls=%fused_computation.28 | convolution fusion | flops 3221749760 | bytes 14155776 | tf_op jit(solution)/shard_map/dot_general | solution.py:376
  358.0 0.0 all-to-all-done.3
  358.0 3.7 all-to-all-start.2
  361.7 0.0 copy-start.3
  361.7 9.0 %fusion.29 = bf16[512,512]{1,0:T(8,128)(2,1)} fusion(bf16[1,512,6144]{2,1,0:T(8,128)(2,1)} %param.13, bf16[3,512,6144]{2,1,0:T(8,128)(2,1)} %get-tuple-element.7), kind=kOutput, calls=%fused_computation.29 | convolution fusion | flops 3221487616 | bytes 13107200 | tf_op jit(solution)/shard_map/dot_general | solution.py:373
  370.7 0.0 all-to-all-done.2
  370.7 4.2 %all-to-all-start.1 = ((bf16[4,128,512]{2,1,0:T(8,128)(2,1)}), bf16[4,128,512]{2,1,0:T(8,128)(2,1)S(1)}, u32[]{:S(2)}, u32[]{:S(2)}) async-start(bf16[4,128,512]{2,1,0:T(8,128)(2,1)} %bitcast.5), calls=%async_computation.1 | async-start | bytes 1048576 | tf_op jit(solution)/shard_map/all_to_all | solution.py:341
  374.9 0.6 broadcast_compare_fusion
  375.5 0.7 reduce_sum.32
  376.2 6.7 %all-to-all-done.1 = bf16[4,128,512]{2,1,0:T(8,128)(2,1)S(1)} async-done(((bf16[4,128,512]{2,1,0:T(8,128)(2,1)}), bf16[4,128,512]{2,1,0:T(8,128)(2,1)S(1)}, u32[]{:S(2)}, u32[]{:S(2)}) %all-to-all-start.1) | async-done | bytes 524320 | tf_op jit(solution)/shard_map/all_to_all | solution.py:341
  382.9 1.5 multiply_reduce_fusion
  384.4 0.0 all-gather.7.cloned.1.call-done
  384.4 0.0 copy-done.3
  384.5 0.0 copy-start.2
  384.5 8.6 %fusion.15 = bf16[1,4096,768]{2,1,0:T(8,128)(2,1)} fusion(bf16[512,4096]{1,0:T(8,128)(2,1)} %all-gather.7.cloned.1.call-done, pred[512]{0:T(512)(128)(4,1)S(1)} %broadcast_compare_fusion, bf16[3,512,768]{2,1,0:T(8,128)(2,1)S(1)} %copy-done.3), kind=kOutput, calls=%fused_computation.22 | convolution fusion | flops 3226468352 | bytes 11272704 | tf_op jit(solution)/shard_map/dot_general | solution.py:399
  393.1 0.0 copy-done.2
  393.1 5.6 %fusion.16 = bf16[1,4096,768]{2,1,0:T(8,128)(2,1)} fusion(bf16[512,4096]{1,0:T(8,128)(2,1)S(1)} %copy-done.2, pred[512]{0:T(512)(128)(4,1)S(1)} %broadcast_compare_fusion, bf16[3,512,768]{2,1,0:T(8,128)(2,1)S(1)} %copy-done.3), kind=kOutput, calls=%fused_computation.23 | convolution fusion | flops 3226468352 | bytes 11272704 | tf_op jit(solution)/shard_map/dot_general | solution.py:399
  398.6 0.0 all-gather.11.cloned.1.call-done
  398.6 8.5 %fusion.17 = bf16[1,4096,768]{2,1,0:T(8,128)(2,1)} fusion(bf16[512,4096]{1,0:T(8,128)(2,1)} %all-gather.11.cloned.1.call-done, f32[512]{0:T(512)} %bitcast.11, bf16[3,512,768]{2,1,0:T(8,128)(2,1)S(1)} %copy-done.3), kind=kOutput, calls=%fused_computation.24 | convolution fusion | flops 3230662656 | bytes 11274240 | tf_op jit(solution)/shard_map/dot_general | solution.py:399
  (1 shorter events, 0.0 us)
Async XLA Ops:
  7.2 27.3 %all-gather.5.cloned.1.call-start = ((), (), s32[]{:S(2)}) async-start(), calls=%async_computation.4 | async-start | bytes 1179648 | tf_op jit(solution)/shard_map/all_gather | solution.py:389
  7.9 74.3 %all-gather.9.cloned.1.call-start = ((), (), s32[]{:S(2)}) async-start(), calls=%async_computation.6 | async-start | bytes 1179648 | tf_op jit(solution)/shard_map/all_gather | solution.py:393
  8.6 375.8 %all-gather.7.cloned.1.call-start = ((), (), s32[]{:S(2)}) async-start(), calls=%async_computation.5 | async-start | bytes 5242880 | tf_op jit(solution)/shard_map/all_gather | solution.py:388
  56.6 301.4 %all-to-all-start.3 = ((f32[4,1,128]{2,1,0:T(1,128)}), f32[4,1,128]{2,1,0:T(1,128)}, u32[]{:S(2)}, u32[]{:S(2)}) async-start(f32[4,1,128]{2,1,0:T(1,128)} %bitcast.10), calls=%async_computation.3 | async-start | bytes 4096 | tf_op jit(solution)/shard_map/all_to_all | solution.py:362
  60.3 338.3 %all-gather.11.cloned.1.call-start = ((), (), s32[]{:S(2)}) async-start(), calls=%async_computation.7 | async-start | bytes 5242880 | tf_op jit(solution)/shard_map/all_gather | solution.py:392
  60.4 16.5 %slice-start = ((s8[6291456]{0:T(1024)(128)(4,1)}), s8[4194304]{0:T(1024)(128)(4,1)S(1)}, s32[]{:S(2)}) async-start(s8[6291456]{0:T(1024)(128)(4,1)} %bitcast.61), calls=%async_computation.8 | async-start | bytes 8388608
  68.6 8.2 %slice-start.1 = ((s8[6291456]{0:T(1024)(128)(4,1)}), s8[2097152]{0:T(1024)(128)(4,1)S(1)}, s32[]{:S(2)}) async-start(s8[6291456]{0:T(1024)(128)(4,1)} %bitcast.61), calls=%async_computation.9 | async-start | bytes 4194304
  82.3 263.2 %copy-start = (bf16[1,512,6144]{2,1,0:T(8,128)(2,1)S(1)}, bf16[1,512,6144]{2,1,0:T(8,128)(2,1)}, u32[]{:S(2)}) copy-start(bf16[1,512,6144]{2,1,0:T(8,128)(2,1)} %param.12) | copy-start | bytes 18874372
  345.4 5.7 %copy-start.1 = (bf16[1,512,6144]{2,1,0:T(8,128)(2,1)S(1)}, bf16[1,512,6144]{2,1,0:T(8,128)(2,1)}, u32[]{:S(2)}) copy-start(bf16[1,512,6144]{2,1,0:T(8,128)(2,1)} %param.11) | copy-start | bytes 18874372
  358.0 12.7 %all-to-all-start.2 = ((bf16[4,128,512]{2,1,0:T(8,128)(2,1)}), bf16[4,128,512]{2,1,0:T(8,128)(2,1)S(1)}, u32[]{:S(2)}, u32[]{:S(2)}) async-start(bf16[4,128,512]{2,1,0:T(8,128)(2,1)} %bitcast.8), calls=%async_computation.2 | async-start | bytes 1048576 | tf_op jit(solution)/shard_map/all_to_all | solution.py:341
  361.7 22.8 %copy-start.3 = (bf16[3,512,768]{2,1,0:T(8,128)(2,1)S(1)}, bf16[3,512,768]{2,1,0:T(8,128)(2,1)}, u32[]{:S(2)}) copy-start(bf16[3,512,768]{2,1,0:T(8,128)(2,1)} %get-tuple-element.8) | copy-start | bytes 7077892
  370.7 12.2 %all-to-all-start.1 = ((bf16[4,128,512]{2,1,0:T(8,128)(2,1)}), bf16[4,128,512]{2,1,0:T(8,128)(2,1)S(1)}, u32[]{:S(2)}, u32[]{:S(2)}) async-start(bf16[4,128,512]{2,1,0:T(8,128)(2,1)} %bitcast.5), calls=%async_computation.1 | async-start | bytes 1048576 | tf_op jit(solution)/shard_map/all_to_all | solution.py:341
  384.5 8.6 %copy-start.2 = (bf16[512,4096]{1,0:T(8,128)(2,1)S(1)}, bf16[512,4096]{1,0:T(8,128)(2,1)}, u32[]{:S(2)}) copy-start(bf16[512,4096]{1,0:T(8,128)(2,1)} %all-gather.7.cloned.1.call-done) | copy-start | bytes 12582916
Sparse Core Ops, SparseCore 0:
  9.6 24.7 all-gather.4
  36.0 21.7 all-gather.8
  59.7 52.2 all-gather.6
  113.6 52.6 all-gather.10

commit v3 on v2

--- a/solution.py
+++ b/solution.py
@@ -9,7 +9,8 @@
 
 MESH = pl.DeviceIdType.MESH
 VMEM_BUDGET = 56 * 1024 * 1024
-BLOCKS = 8
+BLOCKS = 16
+LAG = 2
 
 
 def place(shards):
@@ -233,17 +234,17 @@
         def _():
             relay(i)
 
-        @pl.when(jnp.logical_and(i >= 1, i - 1 < blocks))
-        def _():
-            finish(i - 1)
+        @pl.when(jnp.logical_and(i >= LAG, i - LAG < blocks))
+        def _():
+            finish(i - LAG)
 
         for step in range(1, line):
-            @pl.when(jnp.logical_and(i >= 1 + step, i - 1 - step < blocks))
+            @pl.when(jnp.logical_and(i >= LAG + step, i - LAG - step < blocks))
             def _(step=step):
-                forward(i - 1 - step, step)
+                forward(i - LAG - step, step)
         return carry
 
-    lax.fori_loop(0, blocks + line, advance, 0)
+    lax.fori_loop(0, blocks + LAG + line - 1, advance, 0)
 
     def settle(r, carry):
         keep(r).wait()
@@ -366,9 +367,11 @@
     def partial(rows, weights):
         return jnp.dot(rows, weights, preferred_element_type=jnp.float32).astype(jnp.bfloat16)
 
-    (hidden, d_gate, d_up), (hidden_all, d_gate_all, d_up_all) = to_hidden(
-        (partial(x_part, w_gate), partial(x_part, w_up), partial(dy_part, w_down))
-    )
+    parts = (partial(x_part, w_gate), partial(x_part, w_up), partial(dy_part, w_down))
+    x_home = lax.all_gather(tokens, "shard", axis=1, tiled=True)
+    cot_home = lax.all_gather(cotangent, "shard", axis=1, tiled=True)
+    x_home, cot_home, parts = lax.optimization_barrier((x_home, cot_home, parts))
+    (hidden, d_gate, d_up), (hidden_all, d_gate_all, d_up_all) = to_hidden(parts)
     col_contract = (((1,), (1,)), ((), ()))
     out_rows = lax.dot_general(
         hidden_all, w_down, col_contract, preferred_element_type=jnp.float32
@@ -385,13 +388,9 @@
     )
     grad_tokens = jnp.sum(dx_home.astype(jnp.float32), axis=0).astype(jnp.bfloat16)
 
-    x_rows = lax.all_gather(
-        lax.all_gather(tokens, "shard", axis=1, tiled=True), "expert", axis=0, tiled=True
-    )
+    x_rows = lax.all_gather(x_home, "expert", axis=0, tiled=True)
     x_rows = jnp.where(row_weight > 0, x_rows, jnp.zeros_like(x_rows))
-    cot_rows = lax.all_gather(
-        lax.all_gather(cotangent, "shard", axis=1, tiled=True), "expert", axis=0, tiled=True
-    )
+    cot_rows = lax.all_gather(cot_home, "expert", axis=0, tiled=True)
     dy_rows = (row_weight * cot_rows.astype(jnp.float32)).astype(jnp.bfloat16)
     row_contract = (((0,), (0,)), ((), ()))
 

time: 414 us -> 383 us (0.925)
  blocking collectives: 18 us -> 0 us
  Pallas kernels: 263 us -> 251 us
  waiting for transfers between devices: 33.8 us -> 25.4 us
  starting transfers between devices: 11.8 us -> 17.5 us
    all_gather x4, waiting for transfers between devices: 25.7 us -> 4.03 us  [the longest x1 4.02 us: local(): cot_home = lax.all_gather(cotangent, 'shard', axis=1, tiled=True)]
    all_to_all x1 -> x0, blocking collectives: 18 us -> none  [local(): lax.all_to_all(sent, 'expert', split_axis=0, concat_axis=0, tiled=True)]
    all_to_all x0 -> x1, waiting for transfers between devices: none -> 12.9 us  [local(): lax.all_to_all(sent, 'expert', split_axis=0, concat_axis=0, tiled=True)]
    pallas_call x1, Pallas kernels: 263 us -> 251 us  [exchange(): pl.pallas_call(functools.partial(exchange_kernel, shards, BLOCKS), out_sh...]
    all_to_all x0 -> x1, starting transfers between devices: none -> 5.16 us  [local(): lax.all_to_all(sent, 'expert', split_axis=0, concat_axis=0, tiled=True)]
  transfers between devices with their start and end apart: 7 -> 8, of which waited for: 2 -> 3; matrix products, arithmetic and copies ran while one was open for 16% -> 17% of each run, Pallas kernels for 64% -> 66%
where the time goes in v3:
time: 383 us; the launch traced here: 382 us
  Pallas kernels  251 us (66%)
  matrix products  66.1 us (17%)
  waiting for transfers between devices  25.4 us (7%)
  starting transfers between devices  17.5 us (5%)
  between operations  13.8 us (4%)
  other arithmetic  7.12 us (2%)
    pallas_call x1, Pallas kernels, exchange(): pl.pallas_call(functools.partial(exchange_kernel, shards, BLOCKS), out_sh...  251 us
    dot_general x3, matrix products, gradient(): lax.dot_general(rows, slices, row_contract, preferred_element_type=jnp.fl...  22.7 us
    dot_general x3, matrix products, partial(): jnp.dot(rows, weights, preferred_element_type=jnp.float32)  21.9 us
    all_to_all x1, waiting for transfers between devices, local(): lax.all_to_all(sent, 'expert', split_axis=0, concat_axis=0, tiled=True)  12.9 us
    dot_general x1, matrix products, local(): lax.dot_general(hidden_all, w_down, col_contract, preferred_element_type=...  8.98 us
    all_to_all x2, starting transfers between devices, send_home(): lax.all_to_all(shaped, 'expert', split_axis=0, concat_axis=0, tiled=True)  8.34 us
  transfers between devices with their start and end apart: 8, of which 3 were waited for; matrix products, arithmetic and copies ran while one was open for 17% of the time, Pallas kernels for 66%

profile of v3, /device:TPU:0, one launch (start us, length us, event | category | flops | bytes accessed | tf_op | source)
XLA Modules:
  0.0 382.3 jit_solution(11816767004166424171)
XLA Ops:
  7.2 0.0 all-gather.5.cloned.1.call-start
  7.2 0.7 all-gather.5.cloned.1.call-update
  7.9 0.9 convert_element_type.44
  8.8 1.3 select_reduce_fusion
  10.1 0.8 multiply_convert_fusion.2
  11.0 0.9 broadcast_in_dim.49
  11.9 1.1 pad_maximum_fusion
  13.0 5.2 %all-to-all-start = ((bf16[4,128,1024]{2,1,0:T(8,128)(2,1)}), bf16[4,128,1024]{2,1,0:T(8,128)(2,1)S(1)}, u32[]{:S(2)}, u32[]{:S(2)}) async-start(bf16[4,128,1024]{2,1,0:T(8,128)(2,1)} %pad_maximum_fusion), calls=%async_computation | async-start | bytes 2097152 | tf_op jit(solution)/shard_map/all_to_all | solution.py:360
  18.2 0.0 all-gather.7.cloned.1.call-start
  18.2 0.7 all-gather.7.cloned.1.call-update
  18.9 0.0 all-gather.9.cloned.1.call-start
  18.9 12.9 %all-to-all-done = bf16[4,128,1024]{2,1,0:T(8,128)(2,1)S(1)} async-done(((bf16[4,128,1024]{2,1,0:T(8,128)(2,1)}), bf16[4,128,1024]{2,1,0:T(8,128)(2,1)S(1)}, u32[]{:S(2)}, u32[]{:S(2)}) %all-to-all-start) | async-done | bytes 1048608 | tf_op jit(solution)/shard_map/all_to_all | solution.py:360
  31.8 0.0 slice-start
  31.8 8.2 %convolution_convert_fusion.2.p0 = bf16[512,6144]{1,0:T(8,128)(2,1)} fusion(bf16[1,512,6144]{2,1,0:T(8,128)(2,1)} %param.11, bf16[512,1024]{1,0:T(8,128)(2,1)S(1)} %bitcast.58), kind=kOutput, calls=%fused_computation.2 | convolution fusion | flops 3224371200 | bytes 13107200 | tf_op jit(solution)/shard_map/dot_general | solution.py:368
  40.1 0.0 slice-start.1
  40.1 8.3 %convolution_convert_fusion.1.p1 = bf16[512,6144]{1,0:T(8,128)(2,1)} fusion(bf16[1,512,6144]{2,1,0:T(8,128)(2,1)} %param.12, bf16[512,1024]{1,0:T(8,128)(2,1)S(1)} %bitcast.59), kind=kOutput, calls=%fused_computation.1 | convolution fusion | flops 3224371200 | bytes 13107200 | tf_op jit(solution)/shard_map/dot_general | solution.py:368
  48.3 0.0 slice-done
  48.3 0.0 slice-done.1
  48.4 5.4 %convolution_convert_fusion.p2 = bf16[512,6144]{1,0:T(8,128)(2,1)} fusion(bf16[1,512,6144]{2,1,0:T(8,128)(2,1)S(1)} %bitcast.62, bf16[512,1024]{1,0:T(8,128)(2,1)S(1)} %bitcast.60), kind=kOutput, calls=%fused_computation | convolution fusion | flops 3224371200 | bytes 13107200 | tf_op jit(solution)/shard_map/dot_general | solution.py:368
  53.7 0.0 all-gather.5.cloned.1.call-done
  53.7 4.0 %all-gather.7.cloned.1.call-done = bf16[128,4096]{1,0:T(8,128)(2,1)} async-done(((bf16[128,512]{1,0:T(8,128)(2,1)}), bf16[128,4096]{1,0:T(8,128)(2,1)}) %all-gather.7.cloned.1.call-update) | async-done | bytes 1048592 | tf_op jit(solution)/shard_map/all_gather | solution.py:372
  57.7 0.0 all-gather.9.cloned.1.call-update
  57.8 3.8 %all-to-all-start.3 = ((f32[4,1,128]{2,1,0:T(1,128)}), f32[4,1,128]{2,1,0:T(1,128)}, u32[]{:S(2)}, u32[]{:S(2)}) async-start(f32[4,1,128]{2,1,0:T(1,128)} %bitcast.10), calls=%async_computation.3 | async-start | bytes 4096 | tf_op jit(solution)/shard_map/all_to_all | solution.py:363
  61.6 0.0 all-gather.11.cloned.1.call-start
  61.7 0.5 all-gather.11.cloned.1.call-update
  62.2 0.0 copy-start
  62.2 251.4 %shard_map.110 = (bf16[3,512,768]{2,1,0:T(8,128)(2,1)}, bf16[3,512,6144]{2,1,0:T(8,128)(2,1)}) custom-call(bf16[512,6144]{1,0:T(8,128)(2,1)} %convolution_convert_fusion.2.p0, bf16[512,6144]{1,0:T(8,128)(2,1)} %convolution_convert_fusion.1.p1, bf16[512,6144]{1,0:T(8,128)(2,1)} %convolution_convert_fusion.p2), custom_call_target="tpu_custom_call" | custom-call | flops 199999995904 | bytes 800000000 | tf_op jit(solution)/shard_map/pallas_call | solution.py:279
  313.6 0.0 copy-done
  313.6 0.0 copy-start.1
  313.6 5.7 %fusion = f32[512,512]{1,0:T(8,128)S(1)} fusion(bf16[1,512,6144]{2,1,0:T(8,128)(2,1)S(1)} %copy-done, bf16[3,512,6144]{2,1,0:T(8,128)(2,1)} %get-tuple-element.15), kind=kOutput, calls=%fused_computation.7 | convolution fusion | flops 3221225472 | bytes 13631488 | tf_op jit(solution)/shard_map/dot_general | solution.py:380
  319.4 0.0 copy-done.1
  319.4 6.8 %fusion.24 = bf16[512,512]{1,0:T(8,128)(2,1)} fusion(f32[512,512]{1,0:T(8,128)S(1)} %fusion, bf16[1,512,6144]{2,1,0:T(8,128)(2,1)S(1)} %copy-done.1, bf16[3,512,6144]{2,1,0:T(8,128)(2,1)} %get-tuple-element.15), kind=kOutput, calls=%fused_computation.28 | convolution fusion | flops 3221749760 | bytes 14155776 | tf_op jit(solution)/shard_map/dot_general | solution.py:379
  326.2 0.0 all-to-all-done.3
  326.2 4.1 %all-to-all-start.2 = ((bf16[4,128,512]{2,1,0:T(8,128)(2,1)}), bf16[4,128,512]{2,1,0:T(8,128)(2,1)S(1)}, u32[]{:S(2)}, u32[]{:S(2)}) async-start(bf16[4,128,512]{2,1,0:T(8,128)(2,1)} %bitcast.8), calls=%async_computation.2 | async-start | bytes 1048576 | tf_op jit(solution)/shard_map/all_to_all | solution.py:342
  330.3 0.0 copy-start.3
  330.3 9.0 %fusion.29 = bf16[512,512]{1,0:T(8,128)(2,1)} fusion(bf16[1,512,6144]{2,1,0:T(8,128)(2,1)} %param.13, bf16[3,512,6144]{2,1,0:T(8,128)(2,1)} %get-tuple-element.15), kind=kOutput, calls=%fused_computation.29 | convolution fusion | flops 3221487616 | bytes 13107200 | tf_op jit(solution)/shard_map/dot_general | solution.py:376
  339.3 0.0 all-to-all-done.2
  339.3 4.2 %all-to-all-start.1 = ((bf16[4,128,512]{2,1,0:T(8,128)(2,1)}), bf16[4,128,512]{2,1,0:T(8,128)(2,1)S(1)}, u32[]{:S(2)}, u32[]{:S(2)}) async-start(bf16[4,128,512]{2,1,0:T(8,128)(2,1)} %bitcast.5), calls=%async_computation.1 | async-start | bytes 1048576 | tf_op jit(solution)/shard_map/all_to_all | solution.py:342
  343.5 0.7 broadcast_compare_fusion
  344.2 0.7 reduce_sum.32
  344.9 6.6 %all-to-all-done.1 = bf16[4,128,512]{2,1,0:T(8,128)(2,1)S(1)} async-done(((bf16[4,128,512]{2,1,0:T(8,128)(2,1)}), bf16[4,128,512]{2,1,0:T(8,128)(2,1)S(1)}, u32[]{:S(2)}, u32[]{:S(2)}) %all-to-all-start.1) | async-done | bytes 524320 | tf_op jit(solution)/shard_map/all_to_all | solution.py:342
  351.5 1.6 multiply_reduce_fusion
  353.1 0.0 all-gather.9.cloned.1.call-done
  353.1 0.0 copy-done.3
  353.1 0.0 copy-start.2
  353.1 8.6 %fusion.15 = bf16[1,4096,768]{2,1,0:T(8,128)(2,1)} fusion(bf16[512,4096]{1,0:T(8,128)(2,1)} %all-gather.9.cloned.1.call-done, pred[512]{0:T(512)(128)(4,1)S(1)} %broadcast_compare_fusion, bf16[3,512,768]{2,1,0:T(8,128)(2,1)S(1)} %copy-done.3), kind=kOutput, calls=%fused_computation.22 | convolution fusion | flops 3226468352 | bytes 11272704 | tf_op jit(solution)/shard_map/dot_general | solution.py:398
  361.7 0.0 copy-done.2
  361.7 5.6 %fusion.16 = bf16[1,4096,768]{2,1,0:T(8,128)(2,1)} fusion(bf16[512,4096]{1,0:T(8,128)(2,1)S(1)} %copy-done.2, pred[512]{0:T(512)(128)(4,1)S(1)} %broadcast_compare_fusion, bf16[3,512,768]{2,1,0:T(8,128)(2,1)S(1)} %copy-done.3), kind=kOutput, calls=%fused_computation.23 | convolution fusion | flops 3226468352 | bytes 11272704 | tf_op jit(solution)/shard_map/dot_general | solution.py:398
  367.3 0.0 all-gather.11.cloned.1.call-done
  367.3 8.5 %fusion.17 = bf16[1,4096,768]{2,1,0:T(8,128)(2,1)} fusion(bf16[512,4096]{1,0:T(8,128)(2,1)} %all-gather.11.cloned.1.call-done, f32[512]{0:T(512)} %bitcast.11, bf16[3,512,768]{2,1,0:T(8,128)(2,1)S(1)} %copy-done.3), kind=kOutput, calls=%fused_computation.24 | convolution fusion | flops 3230662656 | bytes 11274240 | tf_op jit(solution)/shard_map/dot_general | solution.py:398
  (1 shorter events, 0.0 us)
Async XLA Ops:
  7.2 46.6 %all-gather.5.cloned.1.call-start = ((), (), s32[]{:S(2)}) async-start(), calls=%async_computation.4 | async-start | bytes 1179648 | tf_op jit(solution)/shard_map/all_gather | solution.py:371
  13.0 18.8 %all-to-all-start = ((bf16[4,128,1024]{2,1,0:T(8,128)(2,1)}), bf16[4,128,1024]{2,1,0:T(8,128)(2,1)S(1)}, u32[]{:S(2)}, u32[]{:S(2)}) async-start(bf16[4,128,1024]{2,1,0:T(8,128)(2,1)} %pad_maximum_fusion), calls=%async_computation | async-start | bytes 2097152 | tf_op jit(solution)/shard_map/all_to_all | solution.py:360
  18.2 39.6 %all-gather.7.cloned.1.call-start = ((), (), s32[]{:S(2)}) async-start(), calls=%async_computation.5 | async-start | bytes 1179648 | tf_op jit(solution)/shard_map/all_gather | solution.py:372
  18.9 334.2 %all-gather.9.cloned.1.call-start = ((), (), s32[]{:S(2)}) async-start(), calls=%async_computation.6 | async-start | bytes 5242880 | tf_op jit(solution)/shard_map/all_gather | solution.py:391
  31.8 16.5 %slice-start = ((s8[6291456]{0:T(1024)(128)(4,1)}), s8[4194304]{0:T(1024)(128)(4,1)S(1)}, s32[]{:S(2)}) async-start(s8[6291456]{0:T(1024)(128)(4,1)} %bitcast.61), calls=%async_computation.8 | async-start | bytes 8388608
  40.1 8.3 %slice-start.1 = ((s8[6291456]{0:T(1024)(128)(4,1)}), s8[2097152]{0:T(1024)(128)(4,1)S(1)}, s32[]{:S(2)}) async-start(s8[6291456]{0:T(1024)(128)(4,1)} %bitcast.61), calls=%async_computation.9 | async-start | bytes 4194304
  57.8 268.4 %all-to-all-start.3 = ((f32[4,1,128]{2,1,0:T(1,128)}), f32[4,1,128]{2,1,0:T(1,128)}, u32[]{:S(2)}, u32[]{:S(2)}) async-start(f32[4,1,128]{2,1,0:T(1,128)} %bitcast.10), calls=%async_computation.3 | async-start | bytes 4096 | tf_op jit(solution)/shard_map/all_to_all | solution.py:363
  61.6 305.7 %all-gather.11.cloned.1.call-start = ((), (), s32[]{:S(2)}) async-start(), calls=%async_computation.7 | async-start | bytes 5242880 | tf_op jit(solution)/shard_map/all_gather | solution.py:393
  62.2 251.4 %copy-start = (bf16[1,512,6144]{2,1,0:T(8,128)(2,1)S(1)}, bf16[1,512,6144]{2,1,0:T(8,128)(2,1)}, u32[]{:S(2)}) copy-start(bf16[1,512,6144]{2,1,0:T(8,128)(2,1)} %param.12) | copy-start | bytes 18874372
  313.6 5.7 %copy-start.1 = (bf16[1,512,6144]{2,1,0:T(8,128)(2,1)S(1)}, bf16[1,512,6144]{2,1,0:T(8,128)(2,1)}, u32[]{:S(2)}) copy-start(bf16[1,512,6144]{2,1,0:T(8,128)(2,1)} %param.11) | copy-start | bytes 18874372
  326.2 13.1 %all-to-all-start.2 = ((bf16[4,128,512]{2,1,0:T(8,128)(2,1)}), bf16[4,128,512]{2,1,0:T(8,128)(2,1)S(1)}, u32[]{:S(2)}, u32[]{:S(2)}) async-start(bf16[4,128,512]{2,1,0:T(8,128)(2,1)} %bitcast.8), calls=%async_computation.2 | async-start | bytes 1048576 | tf_op jit(solution)/shard_map/all_to_all | solution.py:342
  330.3 22.7 %copy-start.3 = (bf16[3,512,768]{2,1,0:T(8,128)(2,1)S(1)}, bf16[3,512,768]{2,1,0:T(8,128)(2,1)}, u32[]{:S(2)}) copy-start(bf16[3,512,768]{2,1,0:T(8,128)(2,1)} %get-tuple-element.17) | copy-start | bytes 7077892
  339.3 12.2 %all-to-all-start.1 = ((bf16[4,128,512]{2,1,0:T(8,128)(2,1)}), bf16[4,128,512]{2,1,0:T(8,128)(2,1)S(1)}, u32[]{:S(2)}, u32[]{:S(2)}) async-start(bf16[4,128,512]{2,1,0:T(8,128)(2,1)} %bitcast.5), calls=%async_computation.1 | async-start | bytes 1048576 | tf_op jit(solution)/shard_map/all_to_all | solution.py:342
  353.1 8.6 %copy-start.2 = (bf16[512,4096]{1,0:T(8,128)(2,1)S(1)}, bf16[512,4096]{1,0:T(8,128)(2,1)}, u32[]{:S(2)}) copy-start(bf16[512,4096]{1,0:T(8,128)(2,1)} %all-gather.9.cloned.1.call-done) | copy-start | bytes 12582916
Sparse Core Ops, SparseCore 0:
  9.6 24.8 all-gather.4
  36.1 21.6 all-gather.6
  59.6 52.2 all-gather.8
  113.6 52.6 all-gather.10

commit v4 on v3

--- a/solution.py
+++ b/solution.py
@@ -10,7 +10,7 @@
 MESH = pl.DeviceIdType.MESH
 VMEM_BUDGET = 56 * 1024 * 1024
 BLOCKS = 16
-LAG = 2
+LAG = 1
 
 
 def place(shards):

time: 383 us -> 376 us (0.982)
  Pallas kernels: 251 us -> 245 us
    pallas_call x1, Pallas kernels: 251 us -> 245 us  [exchange(): pl.pallas_call(functools.partial(exchange_kernel, shards, BLOCKS), out_sh...]
  transfers between devices with their start and end apart: 8 -> 8, of which waited for: 3 -> 3; matrix products, arithmetic and copies ran while one was open for 17% -> 17% of each run, Pallas kernels for 66% -> 65%
where the time goes in v4:
time: 376 us
  Pallas kernels  245 us (65%)
  matrix products  66.1 us (18%)
  waiting for transfers between devices  25.4 us (7%)
  starting transfers between devices  17.5 us (5%)
  between operations  13.8 us (4%)
  other arithmetic  7.12 us (2%)
    pallas_call x1, Pallas kernels, exchange(): pl.pallas_call(functools.partial(exchange_kernel, shards, BLOCKS), out_sh...  245 us
    dot_general x3, matrix products, gradient(): lax.dot_general(rows, slices, row_contract, preferred_element_type=jnp.fl...  22.7 us
    dot_general x3, matrix products, partial(): jnp.dot(rows, weights, preferred_element_type=jnp.float32)  21.9 us
    all_to_all x1, waiting for transfers between devices, local(): lax.all_to_all(sent, 'expert', split_axis=0, concat_axis=0, tiled=True)  12.9 us
    dot_general x1, matrix products, local(): lax.dot_general(hidden_all, w_down, col_contract, preferred_element_type=...  8.98 us
    all_to_all x2, starting transfers between devices, send_home(): lax.all_to_all(shaped, 'expert', split_axis=0, concat_axis=0, tiled=True)  8.33 us
  transfers between devices with their start and end apart: 8, of which 3 were waited for; matrix products, arithmetic and copies ran while one was open for 17% of the time, Pallas kernels for 65%

profile of v4, /device:TPU:0, one launch (start us, length us, event | category | flops | bytes accessed | tf_op | source)
XLA Modules:
  0.0 376.0 jit_solution(6511544766216334278)
XLA Ops:
  7.2 0.0 all-gather.5.cloned.1.call-start
  7.2 0.7 all-gather.5.cloned.1.call-update
  7.9 0.9 convert_element_type.44
  8.8 1.3 select_reduce_fusion
  10.1 0.8 multiply_convert_fusion.2
  11.0 0.9 broadcast_in_dim.49
  11.9 1.1 pad_maximum_fusion
  13.0 5.2 %all-to-all-start = ((bf16[4,128,1024]{2,1,0:T(8,128)(2,1)}), bf16[4,128,1024]{2,1,0:T(8,128)(2,1)S(1)}, u32[]{:S(2)}, u32[]{:S(2)}) async-start(bf16[4,128,1024]{2,1,0:T(8,128)(2,1)} %pad_maximum_fusion), calls=%async_computation | async-start | bytes 2097152 | tf_op jit(solution)/shard_map/all_to_all | solution.py:360
  18.2 0.0 all-gather.7.cloned.1.call-start
  18.2 0.7 all-gather.7.cloned.1.call-update
  18.9 0.0 all-gather.9.cloned.1.call-start
  18.9 12.9 %all-to-all-done = bf16[4,128,1024]{2,1,0:T(8,128)(2,1)S(1)} async-done(((bf16[4,128,1024]{2,1,0:T(8,128)(2,1)}), bf16[4,128,1024]{2,1,0:T(8,128)(2,1)S(1)}, u32[]{:S(2)}, u32[]{:S(2)}) %all-to-all-start) | async-done | bytes 1048608 | tf_op jit(solution)/shard_map/all_to_all | solution.py:360
  31.8 0.0 slice-start
  31.8 8.2 %convolution_convert_fusion.2.p0 = bf16[512,6144]{1,0:T(8,128)(2,1)} fusion(bf16[1,512,6144]{2,1,0:T(8,128)(2,1)} %param.11, bf16[512,1024]{1,0:T(8,128)(2,1)S(1)} %bitcast.58), kind=kOutput, calls=%fused_computation.2 | convolution fusion | flops 3224371200 | bytes 13107200 | tf_op jit(solution)/shard_map/dot_general | solution.py:368
  40.1 0.0 slice-start.1
  40.1 8.3 %convolution_convert_fusion.1.p1 = bf16[512,6144]{1,0:T(8,128)(2,1)} fusion(bf16[1,512,6144]{2,1,0:T(8,128)(2,1)} %param.12, bf16[512,1024]{1,0:T(8,128)(2,1)S(1)} %bitcast.59), kind=kOutput, calls=%fused_computation.1 | convolution fusion | flops 3224371200 | bytes 13107200 | tf_op jit(solution)/shard_map/dot_general | solution.py:368
  48.3 0.0 slice-done
  48.3 0.0 slice-done.1
  48.4 5.4 %convolution_convert_fusion.p2 = bf16[512,6144]{1,0:T(8,128)(2,1)} fusion(bf16[1,512,6144]{2,1,0:T(8,128)(2,1)S(1)} %bitcast.62, bf16[512,1024]{1,0:T(8,128)(2,1)S(1)} %bitcast.60), kind=kOutput, calls=%fused_computation | convolution fusion | flops 3224371200 | bytes 13107200 | tf_op jit(solution)/shard_map/dot_general | solution.py:368
  53.7 0.0 all-gather.5.cloned.1.call-done
  53.7 4.0 %all-gather.7.cloned.1.call-done = bf16[128,4096]{1,0:T(8,128)(2,1)} async-done(((bf16[128,512]{1,0:T(8,128)(2,1)}), bf16[128,4096]{1,0:T(8,128)(2,1)}) %all-gather.7.cloned.1.call-update) | async-done | bytes 1048592 | tf_op jit(solution)/shard_map/all_gather | solution.py:372
  57.7 0.0 all-gather.9.cloned.1.call-update
  57.8 3.8 %all-to-all-start.3 = ((f32[4,1,128]{2,1,0:T(1,128)}), f32[4,1,128]{2,1,0:T(1,128)}, u32[]{:S(2)}, u32[]{:S(2)}) async-start(f32[4,1,128]{2,1,0:T(1,128)} %bitcast.10), calls=%async_computation.3 | async-start | bytes 4096 | tf_op jit(solution)/shard_map/all_to_all | solution.py:363
  61.6 0.0 all-gather.11.cloned.1.call-start
  61.7 0.5 all-gather.11.cloned.1.call-update
  62.2 0.0 copy-start
  62.2 245.1 %shard_map.110 = (bf16[3,512,768]{2,1,0:T(8,128)(2,1)}, bf16[3,512,6144]{2,1,0:T(8,128)(2,1)}) custom-call(bf16[512,6144]{1,0:T(8,128)(2,1)} %convolution_convert_fusion.2.p0, bf16[512,6144]{1,0:T(8,128)(2,1)} %convolution_convert_fusion.1.p1, bf16[512,6144]{1,0:T(8,128)(2,1)} %convolution_convert_fusion.p2), custom_call_target="tpu_custom_call" | custom-call | flops 199999995904 | bytes 800000000 | tf_op jit(solution)/shard_map/pallas_call | solution.py:279
  307.3 0.0 copy-done
  307.3 0.0 copy-start.1
  307.3 5.7 %fusion = f32[512,512]{1,0:T(8,128)S(1)} fusion(bf16[1,512,6144]{2,1,0:T(8,128)(2,1)S(1)} %copy-done, bf16[3,512,6144]{2,1,0:T(8,128)(2,1)} %get-tuple-element.15), kind=kOutput, calls=%fused_computation.7 | convolution fusion | flops 3221225472 | bytes 13631488 | tf_op jit(solution)/shard_map/dot_general | solution.py:380
  313.0 0.0 copy-done.1
  313.0 6.8 %fusion.24 = bf16[512,512]{1,0:T(8,128)(2,1)} fusion(f32[512,512]{1,0:T(8,128)S(1)} %fusion, bf16[1,512,6144]{2,1,0:T(8,128)(2,1)S(1)} %copy-done.1, bf16[3,512,6144]{2,1,0:T(8,128)(2,1)} %get-tuple-element.15), kind=kOutput, calls=%fused_computation.28 | convolution fusion | flops 3221749760 | bytes 14155776 | tf_op jit(solution)/shard_map/dot_general | solution.py:379
  319.8 0.0 all-to-all-done.3
  319.8 4.1 %all-to-all-start.2 = ((bf16[4,128,512]{2,1,0:T(8,128)(2,1)}), bf16[4,128,512]{2,1,0:T(8,128)(2,1)S(1)}, u32[]{:S(2)}, u32[]{:S(2)}) async-start(bf16[4,128,512]{2,1,0:T(8,128)(2,1)} %bitcast.8), calls=%async_computation.2 | async-start | bytes 1048576 | tf_op jit(solution)/shard_map/all_to_all | solution.py:342
  324.0 0.0 copy-start.3
  324.0 9.0 %fusion.29 = bf16[512,512]{1,0:T(8,128)(2,1)} fusion(bf16[1,512,6144]{2,1,0:T(8,128)(2,1)} %param.13, bf16[3,512,6144]{2,1,0:T(8,128)(2,1)} %get-tuple-element.15), kind=kOutput, calls=%fused_computation.29 | convolution fusion | flops 3221487616 | bytes 13107200 | tf_op jit(solution)/shard_map/dot_general | solution.py:376
  333.0 0.0 all-to-all-done.2
  333.0 4.2 %all-to-all-start.1 = ((bf16[4,128,512]{2,1,0:T(8,128)(2,1)}), bf16[4,128,512]{2,1,0:T(8,128)(2,1)S(1)}, u32[]{:S(2)}, u32[]{:S(2)}) async-start(bf16[4,128,512]{2,1,0:T(8,128)(2,1)} %bitcast.5), calls=%async_computation.1 | async-start | bytes 1048576 | tf_op jit(solution)/shard_map/all_to_all | solution.py:342
  337.2 0.7 broadcast_compare_fusion
  337.9 0.7 reduce_sum.32
  338.6 6.6 %all-to-all-done.1 = bf16[4,128,512]{2,1,0:T(8,128)(2,1)S(1)} async-done(((bf16[4,128,512]{2,1,0:T(8,128)(2,1)}), bf16[4,128,512]{2,1,0:T(8,128)(2,1)S(1)}, u32[]{:S(2)}, u32[]{:S(2)}) %all-to-all-start.1) | async-done | bytes 524320 | tf_op jit(solution)/shard_map/all_to_all | solution.py:342
  345.2 1.6 multiply_reduce_fusion
  346.7 0.0 all-gather.9.cloned.1.call-done
  346.7 0.0 copy-done.3
  346.7 0.0 copy-start.2
  346.7 8.6 %fusion.15 = bf16[1,4096,768]{2,1,0:T(8,128)(2,1)} fusion(bf16[512,4096]{1,0:T(8,128)(2,1)} %all-gather.9.cloned.1.call-done, pred[512]{0:T(512)(128)(4,1)S(1)} %broadcast_compare_fusion, bf16[3,512,768]{2,1,0:T(8,128)(2,1)S(1)} %copy-done.3), kind=kOutput, calls=%fused_computation.22 | convolution fusion | flops 3226468352 | bytes 11272704 | tf_op jit(solution)/shard_map/dot_general | solution.py:398
  355.4 0.0 copy-done.2
  355.4 5.6 %fusion.16 = bf16[1,4096,768]{2,1,0:T(8,128)(2,1)} fusion(bf16[512,4096]{1,0:T(8,128)(2,1)S(1)} %copy-done.2, pred[512]{0:T(512)(128)(4,1)S(1)} %broadcast_compare_fusion, bf16[3,512,768]{2,1,0:T(8,128)(2,1)S(1)} %copy-done.3), kind=kOutput, calls=%fused_computation.23 | convolution fusion | flops 3226468352 | bytes 11272704 | tf_op jit(solution)/shard_map/dot_general | solution.py:398
  360.9 0.0 all-gather.11.cloned.1.call-done
  360.9 8.5 %fusion.17 = bf16[1,4096,768]{2,1,0:T(8,128)(2,1)} fusion(bf16[512,4096]{1,0:T(8,128)(2,1)} %all-gather.11.cloned.1.call-done, f32[512]{0:T(512)} %bitcast.11, bf16[3,512,768]{2,1,0:T(8,128)(2,1)S(1)} %copy-done.3), kind=kOutput, calls=%fused_computation.24 | convolution fusion | flops 3230662656 | bytes 11274240 | tf_op jit(solution)/shard_map/dot_general | solution.py:398
  (1 shorter events, 0.0 us)
Async XLA Ops:
  7.2 46.6 %all-gather.5.cloned.1.call-start = ((), (), s32[]{:S(2)}) async-start(), calls=%async_computation.4 | async-start | bytes 1179648 | tf_op jit(solution)/shard_map/all_gather | solution.py:371
  13.0 18.8 %all-to-all-start = ((bf16[4,128,1024]{2,1,0:T(8,128)(2,1)}), bf16[4,128,1024]{2,1,0:T(8,128)(2,1)S(1)}, u32[]{:S(2)}, u32[]{:S(2)}) async-start(bf16[4,128,1024]{2,1,0:T(8,128)(2,1)} %pad_maximum_fusion), calls=%async_computation | async-start | bytes 2097152 | tf_op jit(solution)/shard_map/all_to_all | solution.py:360
  18.2 39.6 %all-gather.7.cloned.1.call-start = ((), (), s32[]{:S(2)}) async-start(), calls=%async_computation.5 | async-start | bytes 1179648 | tf_op jit(solution)/shard_map/all_gather | solution.py:372
  18.9 327.8 %all-gather.9.cloned.1.call-start = ((), (), s32[]{:S(2)}) async-start(), calls=%async_computation.6 | async-start | bytes 5242880 | tf_op jit(solution)/shard_map/all_gather | solution.py:391
  31.8 16.5 %slice-start = ((s8[6291456]{0:T(1024)(128)(4,1)}), s8[4194304]{0:T(1024)(128)(4,1)S(1)}, s32[]{:S(2)}) async-start(s8[6291456]{0:T(1024)(128)(4,1)} %bitcast.61), calls=%async_computation.8 | async-start | bytes 8388608
  40.1 8.3 %slice-start.1 = ((s8[6291456]{0:T(1024)(128)(4,1)}), s8[2097152]{0:T(1024)(128)(4,1)S(1)}, s32[]{:S(2)}) async-start(s8[6291456]{0:T(1024)(128)(4,1)} %bitcast.61), calls=%async_computation.9 | async-start | bytes 4194304
  57.8 262.1 %all-to-all-start.3 = ((f32[4,1,128]{2,1,0:T(1,128)}), f32[4,1,128]{2,1,0:T(1,128)}, u32[]{:S(2)}, u32[]{:S(2)}) async-start(f32[4,1,128]{2,1,0:T(1,128)} %bitcast.10), calls=%async_computation.3 | async-start | bytes 4096 | tf_op jit(solution)/shard_map/all_to_all | solution.py:363
  61.6 299.3 %all-gather.11.cloned.1.call-start = ((), (), s32[]{:S(2)}) async-start(), calls=%async_computation.7 | async-start | bytes 5242880 | tf_op jit(solution)/shard_map/all_gather | solution.py:393
  62.2 245.1 %copy-start = (bf16[1,512,6144]{2,1,0:T(8,128)(2,1)S(1)}, bf16[1,512,6144]{2,1,0:T(8,128)(2,1)}, u32[]{:S(2)}) copy-start(bf16[1,512,6144]{2,1,0:T(8,128)(2,1)} %param.12) | copy-start | bytes 18874372
  307.3 5.7 %copy-start.1 = (bf16[1,512,6144]{2,1,0:T(8,128)(2,1)S(1)}, bf16[1,512,6144]{2,1,0:T(8,128)(2,1)}, u32[]{:S(2)}) copy-start(bf16[1,512,6144]{2,1,0:T(8,128)(2,1)} %param.11) | copy-start | bytes 18874372
  319.8 13.1 %all-to-all-start.2 = ((bf16[4,128,512]{2,1,0:T(8,128)(2,1)}), bf16[4,128,512]{2,1,0:T(8,128)(2,1)S(1)}, u32[]{:S(2)}, u32[]{:S(2)}) async-start(bf16[4,128,512]{2,1,0:T(8,128)(2,1)} %bitcast.8), calls=%async_computation.2 | async-start | bytes 1048576 | tf_op jit(solution)/shard_map/all_to_all | solution.py:342
  324.0 22.8 %copy-start.3 = (bf16[3,512,768]{2,1,0:T(8,128)(2,1)S(1)}, bf16[3,512,768]{2,1,0:T(8,128)(2,1)}, u32[]{:S(2)}) copy-start(bf16[3,512,768]{2,1,0:T(8,128)(2,1)} %get-tuple-element.17) | copy-start | bytes 7077892
  333.0 12.2 %all-to-all-start.1 = ((bf16[4,128,512]{2,1,0:T(8,128)(2,1)}), bf16[4,128,512]{2,1,0:T(8,128)(2,1)S(1)}, u32[]{:S(2)}, u32[]{:S(2)}) async-start(bf16[4,128,512]{2,1,0:T(8,128)(2,1)} %bitcast.5), calls=%async_computation.1 | async-start | bytes 1048576 | tf_op jit(solution)/shard_map/all_to_all | solution.py:342
  346.7 8.6 %copy-start.2 = (bf16[512,4096]{1,0:T(8,128)(2,1)S(1)}, bf16[512,4096]{1,0:T(8,128)(2,1)}, u32[]{:S(2)}) copy-start(bf16[512,4096]{1,0:T(8,128)(2,1)} %all-gather.9.cloned.1.call-done) | copy-start | bytes 12582916
Sparse Core Ops, SparseCore 0:
  9.6 24.8 all-gather.4
  36.1 21.6 all-gather.6
  59.6 52.2 all-gather.8
  113.6 52.6 all-gather.10
